TPU v7x, 32 devices: a whole 2x2x4 slice. The times are simulated.
32 devices in a mesh: sy: 4 (over y, x), sx: 2 (over core), grp: 4 (over z).
Axes of the slice: x: 2, y: 2, z: 4, core: 2. Of those that a mesh axis runs over, the one named last changes fastest.
Arguments:
- image: bfloat16 [4, 64, 128, 256], P('grp', None, 'sy', 'sx'), may hold values from -6 to 6
- weight_one: bfloat16 [3, 3, 64, 64], replicated, may hold values from -0.25 to 0.25
- bias_one: float32 [64], replicated, may hold values from -3 to 3
- weight_two: bfloat16 [3, 3, 64, 64], replicated, may hold values from -0.25 to 0.25
- bias_two: float32 [64], replicated, may hold values from -3 to 3
- cotangent: bfloat16 [4, 64, 128, 256], P('grp', None, 'sy', 'sx'), may hold values from -51 to 51
Outputs:
- output: bfloat16 [4, 64, 128, 256], P('grp', None, 'sy', 'sx')
- image_grad: bfloat16 [4, 64, 128, 256], P('grp', None, 'sy', 'sx')
- grad_weight_one: float32 [3, 3, 64, 64], replicated
- grad_bias_one: float32 [64], replicated
- grad_weight_two: float32 [3, 3, 64, 64], replicated
- grad_bias_two: float32 [64], replicated
All inputs are finite; a program needn't handle non-finite values.
Results may differ from a plain program's by a relative error of at most 0.0075.
Values may be sent and summed in bfloat16 or wider, within the bound.
No kernel may reach another device: no remote copies, remote signals or barrier semaphores. Data moves between devices by JAX's collectives and lax.ppermute only.
A program may use at most 64 MiB of HBM per device.

v0:
```python
import functools

import jax
import jax.numpy as jnp
from jax import lax
from jax.experimental import pallas as pl
from jax.experimental.pallas import tpu as pltpu
from jax.sharding import PartitionSpec as P

BF16 = jnp.bfloat16
F32 = jnp.float32
PARAMS = pltpu.CompilerParams(vmem_limit_bytes=32 * 1024 * 1024)
SWAP = [(0, 1), (1, 0)]
CONTRACT = (((1,), (1,)), ((), ()))
TILES = 37


def shape_of(shape, dtype):
    return jax.ShapeDtypeStruct(shape, dtype)


def near(*arrays):
    return [pltpu.with_memory_space_constraint(array, pltpu.VMEM) for array in arrays]


def far(*arrays):
    return [pltpu.with_memory_space_constraint(array, pltpu.HBM) for array in arrays]


def lasting(micros):
    return pl.CostEstimate(flops=int(micros * 1.1e9), transcendentals=0, bytes_accessed=0)


def turned(side, index, count):
    return index + side * (count - 1 - 2 * index)


def pack_kernel(
    image_ref,
    cot_ref,
    w1,
    b1,
    w2,
    b2,
    image_p,
    cot_p,
    swap,
    edges,
    w1_v,
    b1_v,
    w2_v,
    b2_v,
    image_v,
    cot_v,
    sems,
):
    side = lax.axis_index("sx")
    rows = image_ref.shape[2]
    half = rows // 2
    jobs, small = [], []
    sources = ((image_ref, image_v, image_p), (cot_ref, cot_v, cot_p))
    for c in range(image_ref.shape[1] // 16):
        chans = slice(16 * c, 16 * c + 16)
        for n, (src, dst, out) in enumerate(sources):
            copy = pltpu.make_async_copy(src.at[0, chans], dst.at[chans], sems.at[2 * c + n])
            copy.start()
            jobs.append((copy, chans, dst, out))
    for n, (src, dst) in enumerate(((w1, w1_v), (b1, b1_v), (w2, w2_v), (b2, b2_v))):
        copy = pltpu.make_async_copy(src, dst, sems.at[len(jobs) + n])
        copy.start()
        small.append(copy)
    for copy, chans, dst, out in jobs:
        copy.wait()
        block = jnp.transpose(dst[chans], (1, 0, 2))
        for h in range(rows):
            out[turned(side, h, rows), chans, :] = block[h]
    swap[0 : half + 4] = image_p[half - 4 : rows]
    for k in range(half + 2):
        swap[half + 4 + k] = cot_p[rows - 1 - k]
    for k in range(4):
        edges[k] = image_p[3 - k]
    edges[4:6] = cot_p[0:2]
    for copy in small:
        copy.wait()


def column(row):
    chans = row.shape[1]
    r = lax.broadcasted_iota(jnp.int32, (chans, chans), 0)
    c = lax.broadcasted_iota(jnp.int32, (chans, chans), 1)
    wide = jnp.broadcast_to(row, (chans, chans))
    return jnp.sum(jnp.where(r == c, wide, 0.0), axis=1, keepdims=True)


def weights_kernel(w1, b1, w2, b2, fwd1, fwd2, bwd2, bwd1, bias1, bias2):
    side = lax.axis_index("sx")
    for w, fwd, bwd in ((w1, fwd1, bwd1), (w2, fwd2, bwd2)):
        for a in range(3):
            tap = turned(side, a, 3)
            fwd[a * 64 : a * 64 + 64, :] = jnp.concatenate(
                [jnp.transpose(w[tap, b].astype(F32)) for b in range(3)], axis=1
            ).astype(BF16)
            bwd[a * 64 : a * 64 + 64, :] = jnp.concatenate(
                [w[2 - tap, 2 - b].astype(F32) for b in range(3)], axis=1
            ).astype(BF16)
    bias1[...] = jnp.broadcast_to(column(b1[...]), bias1.shape)
    bias2[...] = jnp.broadcast_to(column(b2[...]), bias2.shape)


def spread(dst, at, row):
    chans, width = row.shape
    zero = jnp.zeros((chans, 1), row.dtype)
    cols = slice(at * width, (at + 1) * width)
    dst[0:chans, cols] = jnp.concatenate([zero, row[:, :-1]], axis=1)
    dst[chans : 2 * chans, cols] = row
    dst[2 * chans : 3 * chans, cols] = jnp.concatenate([row[:, 1:], zero], axis=1)


def sweep(weight_ref, rows, first, emit):
    weight = weight_ref[...]
    upper = lower = None
    for n, (ref, at) in enumerate(rows):
        part = jnp.dot(weight, ref.spread_row(at), preferred_element_type=F32)
        if n >= 2:
            emit(first + n - 1, upper + part[128:192])
        upper = part[64:128] if lower is None else lower + part[64:128]
        lower = part[0:64]


class Rows:
    def __init__(self, ref, width):
        self.ref, self.width = ref, width

    def spread_row(self, at):
        return self.ref[0:192, at * self.width : (at + 1) * self.width]

    def span(self, start, stop):
        return self.ref[:, start * self.width : stop * self.width]


def joined(width, outer, start, inner, split, first, count):
    outer, inner = Rows(outer, width), Rows(inner, width)
    return [
        (outer, e - start) if e < split else (inner, e - split)
        for e in range(first, first + count)
    ]


def silu_and_slope(pre):
    gate = 0.5 + 0.5 * jnp.tanh(0.5 * pre)
    value = pre * gate
    return value, gate + value * (1.0 - gate)


def clear(side, taps, width, start, stop, j0, j1):
    for a in range(3):
        place = pl.ds(pl.multiple_of(64 * turned(side, a, 3), 64), 64)
        for q in range(start, stop):
            if not j0 <= q - a < j1:
                at = q - start
                taps[place, at * width : (at + 1) * width] = jnp.zeros((64, width), BF16)


def store_taps(side, taps, width, start, j, delta):
    for a in range(3):
        place = pl.ds(pl.multiple_of(64 * turned(side, a, 3), 64), 64)
        at = j + a - start
        taps[place, at * width : (at + 1) * width] = delta


def hand_out(side, mine, theirs, at, value):
    width = value.shape[1]
    left, right = value[:, : width // 2], value[:, width // 2 :]
    mine[at] = jnp.where(side == 0, left, right).astype(BF16)
    theirs[at] = jnp.where(side == 0, right, left).astype(BF16)


def inner_kernel(
    image_p,
    cot_p,
    swapped,
    fwd1,
    fwd2,
    bwd2,
    bias1,
    bias2,
    x3,
    h3,
    d3,
    e3,
    slopes,
    mine,
    theirs,
    grad2,
    grad1,
    image_s,
    cot_s,
    taps2,
    taps1,
):
    side = lax.axis_index("sx")
    half = image_p.shape[0] // 2
    width = 2 * image_p.shape[2]
    last = half + 8
    other = 1 - side
    image_s[side] = image_p[0 : half + 4]
    cot_s[side] = cot_p[0 : half + 2]
    for p in range(half + 4):
        image_s[other, p] = swapped[half + 3 - p]
    cot_s[other] = swapped[half + 4 : 2 * half + 6]
    ones = jnp.ones((16, x3.shape[1]), BF16)
    x3[192:208, :] = ones
    h3[192:208, :] = ones[:, : h3.shape[1]]
    clear(side, taps2, width, 2, half + 2, 2, half)
    clear(side, taps1, width, 3, half + 2, 3, half)
    for p in range(half + 4):
        spread(x3, p, jnp.concatenate([image_s[0, p], image_s[1, p]], axis=1))
    shift1 = jnp.broadcast_to(bias1[:, 0:1], (64, width))
    shift2 = jnp.broadcast_to(bias2[:, 0:1], (64, width))

    def first(e, acc):
        hidden, slope = silu_and_slope(acc + shift1)
        spread(h3, e - 5, hidden.astype(BF16))
        if e < half + 5:
            slopes[e - 5] = slope

    x_rows, h_rows = Rows(x3, width), Rows(h3, width)
    sweep(fwd1, [(x_rows, e - 4) for e in range(4, last)], 4, first)

    def second(e, acc):
        value, slope = silu_and_slope(acc + shift2)
        cot = jnp.concatenate([cot_s[0, e - 4], cot_s[1, e - 4]], axis=1).astype(F32)
        delta = (cot * slope).astype(BF16)
        spread(d3, e - 6, delta)
        if e < half + 4:
            hand_out(side, mine, theirs, e - 6, value)
            store_taps(side, taps2, width, 2, e - 4, delta)

    sweep(fwd2, [(h_rows, e - 5) for e in range(5, last - 1)], 5, second)

    def third(e, acc):
        delta = (acc * slopes[e - 5]).astype(BF16)
        spread(e3, e - 7, delta)
        if e < half + 4:
            store_taps(side, taps1, width, 3, e - 4, delta)

    sweep(bwd2, [(Rows(d3, width), e - 6) for e in range(6, last - 2)], 6, third)

    grad2[...] = lax.dot_general(
        h_rows.span(0, half), taps2[...], CONTRACT, preferred_element_type=F32
    )
    grad1[...] = lax.dot_general(
        x_rows.span(2, half + 1), taps1[...], CONTRACT, preferred_element_type=F32
    )


def outer_kernel(
    edges_own,
    edges_other,
    cot_p,
    swapped,
    fwd1,
    fwd2,
    bwd2,
    bias1,
    bias2,
    x3,
    h3,
    d3,
    slopes,
    grad2,
    grad1,
    e3_b,
    mine,
    theirs,
    grads_own,
    grads_send,
    image_s,
    cot_s,
    x3_b,
    h3_b,
    d3_b,
    slopes_b,
    taps2,
    taps1,
):
    side = lax.axis_index("sx")
    place = lax.axis_index("sy")
    half = cot_p.shape[0] // 2
    width = 2 * cot_p.shape[2]
    other = 1 - side
    outside = place == side * (lax.axis_size("sy") - 1)


    def keep(value):
        return jnp.where(outside, 0.0, value.astype(F32)).astype(BF16)

    for half_of, edges in ((side, edges_own), (other, edges_other)):
        image_s[half_of] = keep(edges[0:4])
        cot_s[half_of, 0] = keep(edges[5])
        cot_s[half_of, 1] = keep(edges[4])
    cot_s[side, 2:4] = cot_p[0:2]
    cot_s[other, 2:4] = swapped[half + 4 : half + 6]
    ones = jnp.ones((16, x3_b.shape[1]), BF16)
    x3_b[192:208, :] = ones
    h3_b[192:208, :] = ones
    clear(side, taps2, width, 0, 4, 0, 2)
    clear(side, taps1, width, 0, 5, 0, 3)
    for e in range(4):
        spread(x3_b, e, jnp.concatenate([image_s[0, e], image_s[1, e]], axis=1))
    shift1 = jnp.broadcast_to(bias1[:, 0:1], (64, width))
    shift2 = jnp.broadcast_to(bias2[:, 0:1], (64, width))

    def first(e, acc):
        hidden, slope = silu_and_slope(acc + shift1)
        if e < 4:
            hidden = jnp.where(outside, 0.0, hidden)
        spread(h3_b, e - 1, hidden.astype(BF16))
        if e >= 3:
            slopes_b[e - 3] = slope

    sweep(fwd1, joined(width, x3_b, 0, x3, 4, 0, 6), 0, first)

    def second(e, acc):
        value, slope = silu_and_slope(acc + shift2)
        cot = jnp.concatenate([cot_s[0, e - 2], cot_s[1, e - 2]], axis=1).astype(F32)
        delta = (cot * slope).astype(BF16)
        spread(d3_b, e - 2, delta)
        if e >= 4:
            hand_out(side, mine, theirs, e - 4, value)
            store_taps(side, taps2, width, 0, e - 4, delta)

    sweep(fwd2, joined(width, h3_b, 1, h3, 5, 1, 6), 1, second)

    def third(e, acc):
        delta = acc * (slopes_b[e - 3] if e < 5 else slopes[e - 5])
        if e < 4:
            delta = jnp.where(outside, 0.0, delta)
        delta = delta.astype(BF16)
        spread(e3_b, e - 3, delta)
        if e >= 4:
            store_taps(side, taps1, width, 0, e - 4, delta)

    sweep(bwd2, joined(width, d3_b, 2, d3, 6, 2, 6), 2, third)

    def product(left, right):
        return lax.dot_general(left, right, CONTRACT, preferred_element_type=F32)

    total2 = (
        grad2[...]
        + product(Rows(h3_b, width).span(2, 4), taps2[:, : 2 * width])
        + product(Rows(h3, width).span(0, 2), taps2[:, 2 * width :])
    )
    total1 = (
        grad1[...]
        + product(Rows(x3_b, width).span(3, 4), taps1[:, :width])
        + product(Rows(x3, width).span(0, 4), taps1[:, width:])
    )
    both = jnp.concatenate([total2[0:192], total1[0:192]], axis=1)
    biases = jnp.concatenate([total2[192:200, 64:128], total1[192:200, 64:128]], axis=1)
    tiles = [
        both[8 * (t // 3) : 8 * (t // 3) + 8, 128 * (t % 3) : 128 * (t % 3) + 128]
        for t in range(72)
    ]
    empty = jnp.zeros((8, 128), F32)
    low, high = tiles[:36] + [biases], tiles[36:] + [empty]
    for t in range(TILES):
        at = slice(128 * t, 128 * t + 128)
        grads_own[:, at] = jnp.where(side == 0, low[t], high[t])
        grads_send[:, at] = jnp.where(side == 0, high[t], low[t])


def pair_kernel(own, received, out):
    out[...] = (own[...] + received[...]).astype(BF16)


def add_kernel(factor, *refs):
    out = refs[-1]
    terms = [ref[...].astype(F32) for ref in refs[:-1]]
    while len(terms) > 1:
        terms = [sum(terms[n + 1 : n + 2], terms[n]) for n in range(0, len(terms), 2)]
    out[...] = (terms[0] * factor).astype(out.dtype)


def passing_add(add, passed, *refs):
    add(*refs[:-1])


def behind_add(add, done, *refs):
    add(*refs)


def input_kernel(held, e3_b, e3, bwd1, mine_a, mine_b, theirs_a, theirs_b, mine, theirs):
    side = lax.axis_index("sx")
    half = mine.shape[0] // 2
    width = 2 * mine.shape[2]
    for whole, inner, outer in ((mine, mine_a, mine_b), (theirs, theirs_a, theirs_b)):
        whole[0:2] = outer[...]
        whole[2:half] = inner[...]

    def emit(e, acc):
        hand_out(side, mine, theirs, half + e - 4, acc)

    sweep(bwd1, joined(width, e3_b, 3, e3, 7, 3, half + 2), 3, emit)


def outputs_kernel(mine, back, out, image_grad, token, natural):
    side = lax.axis_index("sx")
    rows = out.shape[2]
    half = rows // 2
    for slot in range(2):
        for j in range(half):
            natural[slot, turned(side, j, rows)] = mine[slot * half + j]
            natural[slot, turned(side, rows - 1 - j, rows)] = back[slot * half + j]
    for slot, ref in ((0, out), (1, image_grad)):
        ref[0] = jnp.transpose(natural[slot], (1, 0, 2))
    token[...] = jnp.zeros(token.shape, F32)


def grads_kernel(held, swapped, gw1, gb1, gw2, gb2):
    side = lax.axis_index("sx")

    def tile(part, t):
        at = slice(128 * t, 128 * t + 128)
        return jnp.where(side == part, held[:, at], swapped[:, at])

    for block in range(24):
        part, first = block // 12, 3 * (block % 12)
        line = jnp.concatenate([tile(part, first + p) for p in range(3)], axis=1)
        b, i = block // 8, (block % 8) * 8
        for a in range(3):
            gw2[a, b, i : i + 8, :] = line[:, a * 64 : a * 64 + 64]
            gw1[a, b, i : i + 8, :] = line[:, 192 + a * 64 : 256 + a * 64]
    biases = tile(0, 36)
    gb2[...] = biases[0:1, 0:64]
    gb1[...] = biases[0:1, 64:128]


def exchange_stages(places, planes):
    def groups(count, axis):
        bits = [1 << k for k in range(count.bit_length() - 1)]
        pairs = [bits[k : k + 2] for k in range(0, len(bits), 2)]
        return [(axis, [b[0]] + ([b[1], b[0] | b[1]] if len(b) == 2 else [])) for b in pairs]

    rows, slides = groups(places, 0), groups(planes, 1)
    stages = []
    for plan in zip(rows + slides, slides + rows):
        stage = []
        for k in range(3):
            pairs = []
            for s in range(places):
                for x, (axis, masks) in enumerate(plan):
                    for g in range(planes):
                        if k < len(masks):
                            t, h = (s ^ masks[k], g) if axis == 0 else (s, g ^ masks[k])
                            pairs.append(((2 * s + x) * planes + g, (2 * t + x) * planes + h))
            if pairs:
                stage.append(pairs)
        stages.append(stage)
    return stages


def local(image, weight_one, bias_one, weight_two, bias_two, cotangent):
    _, chans, rows, cols = image.shape
    places, planes = lax.axis_size("sy"), lax.axis_size("grp")
    half = rows // 2
    width = 2 * cols
    factor = float(rows * cols * places * planes * lax.axis_size("sx")) ** (-0.5)
    call = functools.partial(pl.pallas_call, compiler_params=PARAMS)

    def rows_of(count):
        return pltpu.VMEM((count, chans, cols), BF16)

    def flat(height, count):
        return pltpu.VMEM((height, count * width), BF16)

    image_p, cot_p, swap, edges, w1, b1, w2, b2 = call(
        pack_kernel,
        out_shape=[
            rows_of(rows),
            rows_of(rows),
            rows_of(2 * half + 6),
            rows_of(6),
            pltpu.VMEM(weight_one.shape, BF16),
            pltpu.VMEM((1, chans), F32),
            pltpu.VMEM(weight_two.shape, BF16),
            pltpu.VMEM((1, chans), F32),
        ],
        in_specs=[pl.BlockSpec(memory_space=pltpu.HBM)] * 6,
        scratch_shapes=[
            pltpu.VMEM((chans, rows, cols), BF16),
            pltpu.VMEM((chans, rows, cols), BF16),
            pltpu.SemaphoreType.DMA((chans // 8 + 4,)),
        ],
        name="pack",
    )(
        *far(image, cotangent, weight_one, bias_one.reshape(1, chans)),
        *far(weight_two, bias_two.reshape(1, chans)),
    )
    swapped = lax.ppermute(swap, "sx", SWAP)
    across = []
    for s in range(places):
        upper, lower = 2 * s + 1, 2 * ((s + 1) % places)
        across += [(upper, lower), (lower, upper)]
    edges_other = lax.ppermute(edges, ("sy", "sx"), across)
    edges_own = lax.ppermute(swapped[half : half + 6], ("sy", "sx"), across)
    fwd1, fwd2, bwd2, bwd1, bias1, bias2 = call(
        weights_kernel,
        out_shape=[pltpu.VMEM((192, 192), BF16)] * 4 + [pltpu.VMEM((64, 128), F32)] * 2,
        cost_estimate=lasting(0.3),
        name="weights",
    )(*near(w1, b1, w2, b2))

    x3, h3, d3, e3, slopes, mine_a, theirs_a, grad2, grad1 = call(
        inner_kernel,
        out_shape=[
            flat(208, half + 4),
            flat(208, half + 2),
            flat(192, half),
            flat(192, half - 2),
            pltpu.VMEM((half, chans, width), F32),
            rows_of(half - 2),
            rows_of(half - 2),
            pltpu.VMEM((208, 192), F32),
            pltpu.VMEM((208, 192), F32),
        ],
        scratch_shapes=[
            pltpu.VMEM((2, half + 4, chans, cols), BF16),
            pltpu.VMEM((2, half + 2, chans, cols), BF16),
            flat(192, half),
            flat(192, half - 1),
        ],
        cost_estimate=lasting(4.0),
        name="inner",
    )(*near(image_p, cot_p, swapped, fwd1, fwd2, bwd2, bias1, bias2))
    half_grads = pltpu.VMEM((8, TILES * 128), F32)
    e3_b, mine_b, theirs_b, grads_own, grads_send = call(
        outer_kernel,
        out_shape=[flat(192, 4), rows_of(2), rows_of(2), half_grads, half_grads],
        scratch_shapes=[
            pltpu.VMEM((2, 4, chans, cols), BF16),
            pltpu.VMEM((2, 4, chans, cols), BF16),
            flat(208, 4),
            flat(208, 4),
            flat(192, 4),
            pltpu.VMEM((2, chans, width), F32),
            flat(192, 4),
            flat(192, 5),
        ],
        cost_estimate=lasting(2.0),
        name="outer",
    )(
        *near(edges_own, edges_other, cot_p, swapped, fwd1, fwd2, bwd2, bias1, bias2),
        *near(x3, h3, d3, slopes, grad2, grad1),
    )
    grads_received = lax.ppermute(grads_send, "sx", SWAP)
    held = call(pair_kernel, out_shape=pltpu.VMEM((8, TILES * 128), BF16), name="pair")(
        *near(grads_own, grads_received)
    )
    stages = exchange_stages(places, planes)
    for n, stage in enumerate(stages):
        final = n == len(stages) - 1
        received = [lax.ppermute(held, ("sy", "sx", "grp"), pairs) for pairs in stage]
        sums = pltpu.VMEM((8, TILES * 128), F32 if final else BF16)
        add = functools.partial(add_kernel, factor if final else 1.0)
        if n == 0:
            mine, theirs = call(
                input_kernel,
                out_shape=[rows_of(rows), rows_of(rows)],
                cost_estimate=lasting(1.0),
                name="input",
            )(*near(held, e3_b, e3, bwd1, mine_a, mine_b, theirs_a, theirs_b))
            held, theirs = call(
                functools.partial(passing_add, add),
                out_shape=[sums, rows_of(rows)],
                input_output_aliases={0: 1},
                name="add",
            )(*near(theirs, held, *received))
            back = lax.ppermute(theirs, "sx", SWAP)
            out, image_grad, done = call(
                outputs_kernel,
                out_shape=[shape_of(image.shape, BF16)] * 2 + [pltpu.VMEM((8, 128), F32)],
                scratch_shapes=[pltpu.VMEM((2, rows, chans, cols), BF16)],
                cost_estimate=lasting(1.3),
                name="outputs",
            )(*near(mine, back))
        elif n == 1:
            held = call(functools.partial(behind_add, add), out_shape=sums, name="add")(
                *near(done, held, *received)
            )
        else:
            held = call(add, out_shape=sums, name="add")(*near(held, *received))
    swapped_sums = lax.ppermute(held, "sx", SWAP)
    weight_shape = shape_of((3, 3, chans, chans), F32)
    bias_shape = shape_of((1, chans), F32)
    gw1, gb1, gw2, gb2 = call(
        grads_kernel,
        out_shape=[weight_shape, bias_shape, weight_shape, bias_shape],
        name="grads",
    )(*near(held, swapped_sums))
    return out, image_grad, gw1, gb1.reshape(chans), gw2, gb2.reshape(chans)


def solution(mesh):
    return jax.shard_map(
        local,
        mesh=mesh,
        in_specs=(P("grp", None, "sy", "sx"), P(), P(), P(), P(), P("grp", None, "sy", "sx")),
        out_specs=(P("grp", None, "sy", "sx"), P("grp", None, "sy", "sx"), P(), P(), P(), P()),
        check_vma=False,
    )
```

profile of v0, /device:TPU:0, one launch (start us, length us, event | category | flops | bytes accessed | tf_op | source)
XLA Modules:
  0.0 33.5 jit_solution(13221114754717964380)
XLA Ops:
  0.6 1.5 %pack.1 = (bf16[32,64,128]{2,1,0:T(8,128)(2,1)S(1)}, bf16[32,64,128]{2,1,0:T(8,128)(2,1)S(1)}, bf16[38,64,128]{2,1,0:T(8,128)(2,1)S(1)}, bf16[6,64,128]{2,1,0:T(...) custom-call(bf16[1,64,32,128]{3,2,1,0:T(8,128)(2,1)} %image_ref.1, ...), custom_call_target="tpu_custom_call" | custom-call | tf_op jit(solution)/shard_map/pack/pallas_call | solution.py:477
  2.2 0.5 %collective-permute-start = (bf16[38,64,128]{2,1,0:T(8,128)(2,1)S(1)}, bf16[38,64,128]{2,1,0:T(8,128)(2,1)S(1)}, u32[]{:S(2)}, u32[]{:S(2)}) collective-permute-start(bf16[38,64,128]{2,1,0:T(8,128)(2,1)S(1)} %get-tuple-element.45), channel_id=1, source_target_pairs={{0,4},{4,0},{1,5},{5,1},{2,6},{6,2},{3,7},{7,3},{8,12},{12,8},{9,1... | collective-permute-start | bytes 1867784 | tf_op jit(solution)/shard_map/ppermute | solution.py:500
  2.7 3.6 %collective-permute-start.2 = (bf16[6,64,128]{2,1,0:T(8,128)(2,1)S(1)}, bf16[6,64,128]{2,1,0:T(8,128)(2,1)S(1)}, u32[]{:S(2)}, u32[]{:S(2)}) collective-permute-start(bf16[6,64,128]{2,1,0:T(8,128)(2,1)S(1)} %get-tuple-element.46), channel_id=1, source_target_pairs={{4,8},{8,4},{12,16},{16,12},{20,24},{24,20},{28,0},{0,28},{5,9},{9... | collective-permute-start | bytes 294920 | tf_op jit(solution)/shard_map/ppermute | solution.py:505
  6.2 0.3 weights.1
  6.6 1.4 %collective-permute-start.1 = (bf16[6,64,128]{2,1,0:T(8,128)(2,1)S(1)}, bf16[6,64,128]{2,1,0:T(8,128)(2,1)S(1)}, u32[]{:S(2)}, u32[]{:S(2)}) collective-permute-start(bf16[6,64,128]{2,1,0:T(8,128)(2,1)S(1)} %slice.4), channel_id=1, source_target_pairs={{4,8},{8,4},{12,16},{16,12},{20,24},{24,20},{28,0},{0,28},{5,9},{9... | collective-permute-start | bytes 294920 | tf_op jit(solution)/shard_map/ppermute | solution.py:506
  8.0 3.4 %inner.1 = (bf16[208,5120]{1,0:T(8,128)(2,1)S(1)}, bf16[208,4608]{1,0:T(8,128)(2,1)S(1)}, bf16[192,4096]{1,0:T(8,128)(2,1)S(1)}, bf16[192,3584]{1,0:T(8,128)(2,1...) custom-call(bf16[32,64,128]{2,1,0:T(8,128)(2,1)S(1)} %get-tuple-elem, ...), custom_call_target="tpu_custom_call" | custom-call | flops 4400000000 | tf_op jit(solution)/shard_map/inner/pallas_call | solution.py:514
  11.4 0.7 %collective-permute-done.1.edges_own = bf16[6,64,128]{2,1,0:T(8,128)(2,1)S(1)} collective-permute-done((bf16[6,64,128]{2,1,0:T(8,128)(2,1)S(1)}, bf16[6,64,128]{2,1,0:T(8,128)(2,1)S(1)}, u32[]{:S(2)}, u32[]{:S(2)}) %collective-permute-start.1) | collective-permute-done | bytes 98336 | tf_op jit(solution)/shard_map/ppermute | solution.py:506
  12.1 1.7 %outer.1 = (bf16[192,1024]{1,0:T(8,128)(2,1)S(1)}, bf16[2,64,128]{2,1,0:T(8,128)(2,1)S(1)}, bf16[2,64,128]{2,1,0:T(8,128)(2,1)S(1)}, f32[8,4736]{1,0:T(8,128)S(1)}, f32[8,4736]{1,0:T(8,128)S(1)}) custom-call(bf16[6,64,128]{2,1,0:T(8,128)(2,1)S(1)} %collective-permute-done.1.edges_own, bf16[6,64,128]{2,1,0:T(8,128)(2,1)S(1)} %collective-permute-done.2.edges_other, ...), custom_call_target="tpu_custom_call" | custom-call | flops 2200000000 | tf_op jit(solution)/shard_map/outer/pallas_call | solution.py:537
  13.9 1.4 %collective-permute-done.3.received = f32[8,4736]{1,0:T(8,128)S(1)} collective-permute-done((f32[8,4736]{1,0:T(8,128)S(1)}, f32[8,4736]{1,0:T(8,128)S(1)}, u32[]{:S(2)}, u32[]{:S(2)}) %collective-permute-start.3) | collective-permute-done | bytes 151584 | tf_op jit(solution)/shard_map/ppermute | solution.py:556
  15.3 1.2 %collective-permute-start.6 = (bf16[8,4736]{1,0:T(8,128)(2,1)S(1)}, bf16[8,4736]{1,0:T(8,128)(2,1)S(1)}, u32[]{:S(2)}, u32[]{:S(2)}) collective-permute-start(bf16[8,4736]{1,0:T(8,128)(2,1)S(1)} %pair.1.held.refs_0_), channel_id=1, source_target_pairs={{0,24},{1,25},{2,26},{3,27},{4,7},{5,6},{6,5},{7,4},{8,16},{9,17},... | collective-permute-start | bytes 227336 | tf_op jit(solution)/shard_map/ppermute | solution.py:563
  16.5 1.0 %collective-permute-start.5 = (bf16[8,4736]{1,0:T(8,128)(2,1)S(1)}, bf16[8,4736]{1,0:T(8,128)(2,1)S(1)}, u32[]{:S(2)}, u32[]{:S(2)}) collective-permute-start(bf16[8,4736]{1,0:T(8,128)(2,1)S(1)} %pair.1.held.refs_0_), channel_id=1, source_target_pairs={{0,16},{1,17},{2,18},{3,19},{4,6},{5,7},{6,4},{7,5},{8,24},{9,25},... | collective-permute-start | bytes 227336 | tf_op jit(solution)/shard_map/ppermute | solution.py:563
  17.5 1.3 %collective-permute-start.4 = (bf16[8,4736]{1,0:T(8,128)(2,1)S(1)}, bf16[8,4736]{1,0:T(8,128)(2,1)S(1)}, u32[]{:S(2)}, u32[]{:S(2)}) collective-permute-start(bf16[8,4736]{1,0:T(8,128)(2,1)S(1)} %pair.1.held.refs_0_), channel_id=1, source_target_pairs={{0,8},{1,9},{2,10},{3,11},{4,5},{5,4},{6,7},{7,6},{8,0},{9,1},{10,... | collective-permute-start | bytes 227336 | tf_op jit(solution)/shard_map/ppermute | solution.py:563
  18.8 0.6 %input.1 = (bf16[32,64,128]{2,1,0:T(8,128)(2,1)S(1)}, bf16[32,64,128]{2,1,0:T(8,128)(2,1)S(1)}) custom-call(bf16[8,4736]{1,0:T(8,128)(2,1)S(1)} %pair.1.held.refs_0_, bf16[192,1024]{1,0:T(8,128)(2,1)S(1)} %get-tuple-element.66.e3_b, bf16[192,3584]{1,0:T(8,128)(2,1)S(1)} %get-tuple-element.67.e3, bf16[192,192]{1,0:T(8,128)(2,1)S(1)} %get-tuple-element.68.bwd1, ...), custom_call_target="tpu_custom_call" | custom-call | flops 1100000000 | tf_op jit(solution)/shard_map/input/pallas_call | solution.py:567
  19.5 1.2 %collective-permute-done.6.refs_3_ = bf16[8,4736]{1,0:T(8,128)(2,1)S(1)} collective-permute-done((bf16[8,4736]{1,0:T(8,128)(2,1)S(1)}, bf16[8,4736]{1,0:T(8,128)(2,1)S(1)}, u32[]{:S(2)}, u32[]{:S(2)}) %collective-permute-start.6) | collective-permute-done | bytes 75808 | tf_op jit(solution)/shard_map/ppermute | solution.py:563
  20.7 0.8 %collective-permute-done.5.refs_2_ = bf16[8,4736]{1,0:T(8,128)(2,1)S(1)} collective-permute-done((bf16[8,4736]{1,0:T(8,128)(2,1)S(1)}, bf16[8,4736]{1,0:T(8,128)(2,1)S(1)}, u32[]{:S(2)}, u32[]{:S(2)}) %collective-permute-start.5) | collective-permute-done | bytes 75808 | tf_op jit(solution)/shard_map/ppermute | solution.py:563
  21.4 0.5 %collective-permute-done.4.refs_1_ = bf16[8,4736]{1,0:T(8,128)(2,1)S(1)} collective-permute-done((bf16[8,4736]{1,0:T(8,128)(2,1)S(1)}, bf16[8,4736]{1,0:T(8,128)(2,1)S(1)}, u32[]{:S(2)}, u32[]{:S(2)}) %collective-permute-start.4) | collective-permute-done | bytes 75808 | tf_op jit(solution)/shard_map/ppermute | solution.py:563
  22.0 1.1 %collective-permute-start.7 = (bf16[32,64,128]{2,1,0:T(8,128)(2,1)S(1)}, bf16[32,64,128]{2,1,0:T(8,128)(2,1)S(1)}, u32[]{:S(2)}, u32[]{:S(2)}) collective-permute-start(bf16[32,64,128]{2,1,0:T(8,128)(2,1)S(1)} %get-tuple-element.75), channel_id=1, source_target_pairs={{0,4},{4,0},{1,5},{5,1},{2,6},{6,2},{3,7},{7,3},{8,12},{12,8},{9,1... | collective-permute-start | bytes 1572872 | tf_op jit(solution)/shard_map/ppermute | solution.py:579
  23.1 2.7 %collective-permute-start.10 = (bf16[8,4736]{1,0:T(8,128)(2,1)S(1)}, bf16[8,4736]{1,0:T(8,128)(2,1)S(1)}, u32[]{:S(2)}, u32[]{:S(2)}) collective-permute-start(bf16[8,4736]{1,0:T(8,128)(2,1)S(1)} %get-tuple-element.79.refs_0_), channel_id=1, source_target_pairs={{0,3},{1,2},{2,1},{3,0},{4,28},{5,29},{6,30},{7,31},{8,11},{9,10},... | collective-permute-start | bytes 227336 | tf_op jit(solution)/shard_map/ppermute | solution.py:563
  25.7 1.7 %collective-permute-start.8 = (bf16[8,4736]{1,0:T(8,128)(2,1)S(1)}, bf16[8,4736]{1,0:T(8,128)(2,1)S(1)}, u32[]{:S(2)}, u32[]{:S(2)}) collective-permute-start(bf16[8,4736]{1,0:T(8,128)(2,1)S(1)} %get-tuple-element.79.refs_0_), channel_id=1, source_target_pairs={{0,1},{1,0},{2,3},{3,2},{4,12},{5,13},{6,14},{7,15},{8,9},{9,8},{1... | collective-permute-start | bytes 227336 | tf_op jit(solution)/shard_map/ppermute | solution.py:563
  27.4 1.3 %outputs.1 = (bf16[1,64,32,128]{3,2,1,0:T(8,128)(2,1)}, bf16[1,64,32,128]{3,2,1,0:T(8,128)(2,1)}, f32[8,128]{1,0:T(8,128)S(1)}) custom-call(bf16[32,64,128]{2,1,0:T(8,128)(2,1)S(1)} %get-tuple-element.73.mine, bf16[32,64,128]{2,1,0:T(8,128)(2,1)S(1)} %collective-permute-done.7.back), custom_call_target="tpu_custom_call" | custom-call | flops 1430000000 | tf_op jit(solution)/shard_map/outputs/pallas_call | solution.py:580
  28.7 0.5 %collective-permute-done.10.refs_3_ = bf16[8,4736]{1,0:T(8,128)(2,1)S(1)} collective-permute-done((bf16[8,4736]{1,0:T(8,128)(2,1)S(1)}, bf16[8,4736]{1,0:T(8,128)(2,1)S(1)}, u32[]{:S(2)}, u32[]{:S(2)}) %collective-permute-start.10) | collective-permute-done | bytes 75808 | tf_op jit(solution)/shard_map/ppermute | solution.py:563
  29.2 1.8 %collective-permute-done.9.refs_2_ = bf16[8,4736]{1,0:T(8,128)(2,1)S(1)} collective-permute-done((bf16[8,4736]{1,0:T(8,128)(2,1)S(1)}, bf16[8,4736]{1,0:T(8,128)(2,1)S(1)}, u32[]{:S(2)}, u32[]{:S(2)}) %collective-permute-start.9) | collective-permute-done | bytes 75808 | tf_op jit(solution)/shard_map/ppermute | solution.py:563
  31.1 1.4 %collective-permute-done.11.swapped = f32[8,4736]{1,0:T(8,128)S(1)} collective-permute-done((f32[8,4736]{1,0:T(8,128)S(1)}, f32[8,4736]{1,0:T(8,128)S(1)}, u32[]{:S(2)}, u32[]{:S(2)}) %collective-permute-start.11) | collective-permute-done | bytes 151584 | tf_op jit(solution)/shard_map/ppermute | solution.py:593
  32.5 1.0 %grads.1 = (f32[3,3,64,64]{3,2,1,0:T(8,128)}, f32[1,64]{1,0:T(1,128)}, f32[3,3,64,64]{3,2,1,0:T(8,128)}, f32[1,64]{1,0:T(1,128)}) custom-call(f32[8,4736]{1,0:T(8,128)S(1)} %add.3.held, f32[8,4736]{1,0:T(8,128)S(1)} %collective-permute-done.11.swapped), custom_call_target="tpu_custom_call" | custom-call | tf_op jit(solution)/shard_map/grads/pallas_call | solution.py:596
  (11 shorter events, 0.3 us)
Async XLA Ops:
  2.2 4.4 %collective-permute-start = (bf16[38,64,128]{2,1,0:T(8,128)(2,1)S(1)}, bf16[38,64,128]{2,1,0:T(8,128)(2,1)S(1)}, u32[]{:S(2)}, u32[]{:S(2)}) collective-permute-start(bf16[38,64,128]{2,1,0:T(8,128)(2,1)S(1)} %get-tuple-element.45), channel_id=1, source_target_pairs={{0,4},{4,0},{1,5},{5,1},{2,6},{6,2},{3,7},{7,3},{8,12},{12,8},{9,1... | collective-permute-start | bytes 1867784 | tf_op jit(solution)/shard_map/ppermute | solution.py:500
  2.7 8.7 %collective-permute-start.2 = (bf16[6,64,128]{2,1,0:T(8,128)(2,1)S(1)}, bf16[6,64,128]{2,1,0:T(8,128)(2,1)S(1)}, u32[]{:S(2)}, u32[]{:S(2)}) collective-permute-start(bf16[6,64,128]{2,1,0:T(8,128)(2,1)S(1)} %get-tuple-element.46), channel_id=1, source_target_pairs={{4,8},{8,4},{12,16},{16,12},{20,24},{24,20},{28,0},{0,28},{5,9},{9... | collective-permute-start | bytes 294920 | tf_op jit(solution)/shard_map/ppermute | solution.py:505
  6.6 5.6 %collective-permute-start.1 = (bf16[6,64,128]{2,1,0:T(8,128)(2,1)S(1)}, bf16[6,64,128]{2,1,0:T(8,128)(2,1)S(1)}, u32[]{:S(2)}, u32[]{:S(2)}) collective-permute-start(bf16[6,64,128]{2,1,0:T(8,128)(2,1)S(1)} %slice.4), channel_id=1, source_target_pairs={{4,8},{8,4},{12,16},{16,12},{20,24},{24,20},{28,0},{0,28},{5,9},{9... | collective-permute-start | bytes 294920 | tf_op jit(solution)/shard_map/ppermute | solution.py:506
  13.8 1.4 %collective-permute-start.3 = (f32[8,4736]{1,0:T(8,128)S(1)}, f32[8,4736]{1,0:T(8,128)S(1)}, u32[]{:S(2)}, u32[]{:S(2)}) collective-permute-start(f32[8,4736]{1,0:T(8,128)S(1)} %get-tuple-element.65), channel_id=1, source_target_pairs={{0,4},{4,0},{1,5},{5,1},{2,6},{6,2},{3,7},{7,3},{8,12},{12,8},{9,1... | collective-permute-start | bytes 454664 | tf_op jit(solution)/shard_map/ppermute | solution.py:556
  15.3 5.4 %collective-permute-start.6 = (bf16[8,4736]{1,0:T(8,128)(2,1)S(1)}, bf16[8,4736]{1,0:T(8,128)(2,1)S(1)}, u32[]{:S(2)}, u32[]{:S(2)}) collective-permute-start(bf16[8,4736]{1,0:T(8,128)(2,1)S(1)} %pair.1.held.refs_0_), channel_id=1, source_target_pairs={{0,24},{1,25},{2,26},{3,27},{4,7},{5,6},{6,5},{7,4},{8,16},{9,17},... | collective-permute-start | bytes 227336 | tf_op jit(solution)/shard_map/ppermute | solution.py:563
  16.5 4.9 %collective-permute-start.5 = (bf16[8,4736]{1,0:T(8,128)(2,1)S(1)}, bf16[8,4736]{1,0:T(8,128)(2,1)S(1)}, u32[]{:S(2)}, u32[]{:S(2)}) collective-permute-start(bf16[8,4736]{1,0:T(8,128)(2,1)S(1)} %pair.1.held.refs_0_), channel_id=1, source_target_pairs={{0,16},{1,17},{2,18},{3,19},{4,6},{5,7},{6,4},{7,5},{8,24},{9,25},... | collective-permute-start | bytes 227336 | tf_op jit(solution)/shard_map/ppermute | solution.py:563
  17.5 4.4 %collective-permute-start.4 = (bf16[8,4736]{1,0:T(8,128)(2,1)S(1)}, bf16[8,4736]{1,0:T(8,128)(2,1)S(1)}, u32[]{:S(2)}, u32[]{:S(2)}) collective-permute-start(bf16[8,4736]{1,0:T(8,128)(2,1)S(1)} %pair.1.held.refs_0_), channel_id=1, source_target_pairs={{0,8},{1,9},{2,10},{3,11},{4,5},{5,4},{6,7},{7,6},{8,0},{9,1},{10,... | collective-permute-start | bytes 227336 | tf_op jit(solution)/shard_map/ppermute | solution.py:563
  22.0 5.5 %collective-permute-start.7 = (bf16[32,64,128]{2,1,0:T(8,128)(2,1)S(1)}, bf16[32,64,128]{2,1,0:T(8,128)(2,1)S(1)}, u32[]{:S(2)}, u32[]{:S(2)}) collective-permute-start(bf16[32,64,128]{2,1,0:T(8,128)(2,1)S(1)} %get-tuple-element.75), channel_id=1, source_target_pairs={{0,4},{4,0},{1,5},{5,1},{2,6},{6,2},{3,7},{7,3},{8,12},{12,8},{9,1... | collective-permute-start | bytes 1572872 | tf_op jit(solution)/shard_map/ppermute | solution.py:579
  23.1 6.2 %collective-permute-start.10 = (bf16[8,4736]{1,0:T(8,128)(2,1)S(1)}, bf16[8,4736]{1,0:T(8,128)(2,1)S(1)}, u32[]{:S(2)}, u32[]{:S(2)}) collective-permute-start(bf16[8,4736]{1,0:T(8,128)(2,1)S(1)} %get-tuple-element.79.refs_0_), channel_id=1, source_target_pairs={{0,3},{1,2},{2,1},{3,0},{4,28},{5,29},{6,30},{7,31},{8,11},{9,10},... | collective-permute-start | bytes 227336 | tf_op jit(solution)/shard_map/ppermute | solution.py:563
  25.7 5.3 %collective-permute-start.9 = (bf16[8,4736]{1,0:T(8,128)(2,1)S(1)}, bf16[8,4736]{1,0:T(8,128)(2,1)S(1)}, u32[]{:S(2)}, u32[]{:S(2)}) collective-permute-start(bf16[8,4736]{1,0:T(8,128)(2,1)S(1)} %get-tuple-element.79.refs_0_), channel_id=1, source_target_pairs={{0,2},{1,3},{2,0},{3,1},{4,20},{5,21},{6,22},{7,23},{8,10},{9,11},... | collective-permute-start | bytes 227336 | tf_op jit(solution)/shard_map/ppermute | solution.py:563
  25.7 5.3 %collective-permute-start.8 = (bf16[8,4736]{1,0:T(8,128)(2,1)S(1)}, bf16[8,4736]{1,0:T(8,128)(2,1)S(1)}, u32[]{:S(2)}, u32[]{:S(2)}) collective-permute-start(bf16[8,4736]{1,0:T(8,128)(2,1)S(1)} %get-tuple-element.79.refs_0_), channel_id=1, source_target_pairs={{0,1},{1,0},{2,3},{3,2},{4,12},{5,13},{6,14},{7,15},{8,9},{9,8},{1... | collective-permute-start | bytes 227336 | tf_op jit(solution)/shard_map/ppermute | solution.py:563
  31.0 1.4 %collective-permute-start.11 = (f32[8,4736]{1,0:T(8,128)S(1)}, f32[8,4736]{1,0:T(8,128)S(1)}, u32[]{:S(2)}, u32[]{:S(2)}) collective-permute-start(f32[8,4736]{1,0:T(8,128)S(1)} %add.3.held), channel_id=1, source_target_pairs={{0,4},{4,0},{1,5},{5,1},{2,6},{6,2},{3,7},{7,3},{8,12},{12,8},{9,1... | collective-permute-start | bytes 454664 | tf_op jit(solution)/shard_map/ppermute | solution.py:593
where the time goes:
time: 33.6 us; the launch traced here: 33.5 us
  starting transfers between devices  14.6 us (43%)
  Pallas kernels  9.93 us (30%)
  waiting for transfers between devices  8.16 us (24%)
  between operations  0.73 us (2%)
    ppermute x6, starting transfers between devices, local(): lax.ppermute(held, ('sy', 'sx', 'grp'), pairs)  7.94 us
    ppermute x6, waiting for transfers between devices, local(): lax.ppermute(held, ('sy', 'sx', 'grp'), pairs)  4.71 us
    ppermute x1, starting transfers between devices, local(): edges_other = lax.ppermute(edges, ('sy', 'sx'), across)  3.56 us
    pallas_call x1, Pallas kernels, local(): call(inner_kernel, out_shape=[flat(208, half + 4), flat(208, half + 2), f...  3.44 us
    pallas_call x1, Pallas kernels, local(): call(outer_kernel, out_shape=[flat(192, 4), rows_of(2), rows_of(2), half_...  1.67 us
    pallas_call x1, Pallas kernels, local(): call(pack_kernel, out_shape=[rows_of(rows), rows_of(rows), rows_of(2 * ha...  1.53 us
    ppermute x1, starting transfers between devices, local(): edges_own = lax.ppermute(swapped[half:half + 6], ('sy', 'sx'), across)  1.39 us
    ppermute x1, waiting for transfers between devices, local(): grads_received = lax.ppermute(grads_send, 'sx', SWAP)  1.36 us
  transfers between devices with their start and end apart: 12, of which 8 were waited for; matrix products, arithmetic and copies ran while one was open for 0% of the time, Pallas kernels for 17%

commit v1 on v0

--- a/solution.py
+++ b/solution.py
@@ -52,6 +52,7 @@
     b2_v,
     image_v,
     cot_v,
+    wides,
     sems,
 ):
     side = lax.axis_index("sx")
@@ -69,11 +70,13 @@
         copy = pltpu.make_async_copy(src, dst, sems.at[len(jobs) + n])
         copy.start()
         small.append(copy)
-    for copy, chans, dst, out in jobs:
+    for n, (copy, chans, dst, out) in enumerate(jobs):
         copy.wait()
-        block = jnp.transpose(dst[chans], (1, 0, 2))
+        wide = wides.at[n]
+        wide[...] = dst[chans].astype(F32).reshape(wide.shape)
         for h in range(rows):
-            out[turned(side, h, rows), chans, :] = block[h]
+            row = wide[pl.ds(h, 16, stride=rows), :]
+            out[turned(side, h, rows), chans, :] = row.astype(BF16)
     swap[0 : half + 4] = image_p[half - 4 : rows]
     for k in range(half + 2):
         swap[half + 4 + k] = cot_p[rows - 1 - k]
@@ -490,6 +493,7 @@
         scratch_shapes=[
             pltpu.VMEM((chans, rows, cols), BF16),
             pltpu.VMEM((chans, rows, cols), BF16),
+            pltpu.VMEM((chans // 8, 16 * rows, cols), F32),
             pltpu.SemaphoreType.DMA((chans // 8 + 4,)),
         ],
         name="pack",
@@ -500,10 +504,13 @@
     swapped = lax.ppermute(swap, "sx", SWAP)
     across = []
     for s in range(places):
-        upper, lower = 2 * s + 1, 2 * ((s + 1) % places)
-        across += [(upper, lower), (lower, upper)]
-    edges_other = lax.ppermute(edges, ("sy", "sx"), across)
-    edges_own = lax.ppermute(swapped[half : half + 6], ("sy", "sx"), across)
+        for g in range(planes):
+            lower, upper = 2 * s * planes + g, (2 * s + 1) * planes + g
+            across.append((lower, lower - planes if s > 0 else lower ^ 1))
+            across.append((upper, upper + planes if s < places - 1 else upper ^ 1))
+    axes = ("sy", "sx", "grp")
+    edges_other = lax.ppermute(edges, axes, across)
+    edges_own = lax.ppermute(swapped[half : half + 6], axes, across)
     fwd1, fwd2, bwd2, bwd1, bias1, bias2 = call(
         weights_kernel,
         out_shape=[pltpu.VMEM((192, 192), BF16)] * 4 + [pltpu.VMEM((64, 128), F32)] * 2,
@@ -560,7 +567,7 @@
     stages = exchange_stages(places, planes)
     for n, stage in enumerate(stages):
         final = n == len(stages) - 1
-        received = [lax.ppermute(held, ("sy", "sx", "grp"), pairs) for pairs in stage]
+        received = [lax.ppermute(held, axes, pairs) for pairs in stage]
         sums = pltpu.VMEM((8, TILES * 128), F32 if final else BF16)
         add = functools.partial(add_kernel, factor if final else 1.0)
         if n == 0:

time: 33.6 us -> 34.5 us (1.027)
  starting transfers between devices: 14.6 us -> 13.1 us
  waiting for transfers between devices: 8.16 us -> 9.63 us
  Pallas kernels: 9.93 us -> 10.8 us
    ppermute x8, waiting for transfers between devices: 5.43 us -> 6.93 us  [the longest x6 6.92 us: local(): received = [lax.ppermute(held, axes, pairs) for pairs in stage]]
    ppermute x1, starting transfers between devices: 1.09 us -> 0.07 us  [local(): back = lax.ppermute(theirs, 'sx', SWAP)]
    pallas_call x1, Pallas kernels: 1.53 us -> 2.41 us  [local(): call(pack_kernel, out_shape=[rows_of(rows), rows_of(rows), rows_of(2 * ha...]
    ppermute x8, starting transfers between devices: 12.9 us -> 12.4 us  [the longest x6 8 us: local(): received = [lax.ppermute(held, axes, pairs) for pairs in stage]]
  transfers between devices with their start and end apart: 12 -> 12, of which waited for: 8 -> 7; matrix products, arithmetic and copies ran while one was open for 0% -> 0% of each run, Pallas kernels for 17% -> 16%
where the time goes in v1:
time: 34.5 us; the launch traced here: 34.3 us
  starting transfers between devices  13.1 us (38%)
  Pallas kernels  10.8 us (31%)
  waiting for transfers between devices  9.63 us (28%)
  between operations  0.73 us (2%)
    ppermute x6, starting transfers between devices, local(): received = [lax.ppermute(held, axes, pairs) for pairs in stage]  8 us
    ppermute x6, waiting for transfers between devices, local(): received = [lax.ppermute(held, axes, pairs) for pairs in stage]  6.92 us
    pallas_call x1, Pallas kernels, local(): call(inner_kernel, out_shape=[flat(208, half + 4), flat(208, half + 2), f...  3.44 us
    ppermute x1, starting transfers between devices, local(): edges_other = lax.ppermute(edges, axes, across)  2.65 us
    pallas_call x1, Pallas kernels, local(): call(pack_kernel, out_shape=[rows_of(rows), rows_of(rows), rows_of(2 * ha...  2.41 us
    ppermute x1, starting transfers between devices, local(): edges_own = lax.ppermute(swapped[half:half + 6], axes, across)  1.72 us
    pallas_call x1, Pallas kernels, local(): call(outer_kernel, out_shape=[flat(192, 4), rows_of(2), rows_of(2), half_...  1.69 us
    ppermute x1, waiting for transfers between devices, local(): swapped_sums = lax.ppermute(held, 'sx', SWAP)  1.36 us
  transfers between devices with their start and end apart: 12, of which 7 were waited for; matrix products, arithmetic and copies ran while one was open for 0% of the time, Pallas kernels for 16%

profile of v1, /device:TPU:0, one launch (start us, length us, event | category | flops | bytes accessed | tf_op | source)
XLA Modules:
  0.0 34.3 jit_solution(3363324012204134060)
XLA Ops:
  0.6 2.4 %pack.1 = (bf16[32,64,128]{2,1,0:T(8,128)(2,1)S(1)}, bf16[32,64,128]{2,1,0:T(8,128)(2,1)S(1)}, bf16[38,64,128]{2,1,0:T(8,128)(2,1)S(1)}, bf16[6,64,128]{2,1,0:T(...) custom-call(bf16[1,64,32,128]{3,2,1,0:T(8,128)(2,1)} %image_ref.1, ...), custom_call_target="tpu_custom_call" | custom-call | tf_op jit(solution)/shard_map/pack/pallas_call | solution.py:480
  3.0 0.5 %collective-permute-start = (bf16[38,64,128]{2,1,0:T(8,128)(2,1)S(1)}, bf16[38,64,128]{2,1,0:T(8,128)(2,1)S(1)}, u32[]{:S(2)}, u32[]{:S(2)}) collective-permute-start(bf16[38,64,128]{2,1,0:T(8,128)(2,1)S(1)} %get-tuple-element.45), channel_id=1, source_target_pairs={{0,4},{4,0},{1,5},{5,1},{2,6},{6,2},{3,7},{7,3},{8,12},{12,8},{9,1... | collective-permute-start | bytes 1867784 | tf_op jit(solution)/shard_map/ppermute | solution.py:504
  3.6 2.6 %collective-permute-start.2 = (bf16[6,64,128]{2,1,0:T(8,128)(2,1)S(1)}, bf16[6,64,128]{2,1,0:T(8,128)(2,1)S(1)}, u32[]{:S(2)}, u32[]{:S(2)}) collective-permute-start(bf16[6,64,128]{2,1,0:T(8,128)(2,1)S(1)} %get-tuple-element.46), channel_id=1, source_target_pairs={{0,1},{4,8},{1,0},{5,9},{2,3},{6,10},{3,2},{7,11},{8,4},{12,16},{9... | collective-permute-start | bytes 294920 | tf_op jit(solution)/shard_map/ppermute | solution.py:512
  6.2 0.3 weights.1
  6.5 1.7 %collective-permute-start.1 = (bf16[6,64,128]{2,1,0:T(8,128)(2,1)S(1)}, bf16[6,64,128]{2,1,0:T(8,128)(2,1)S(1)}, u32[]{:S(2)}, u32[]{:S(2)}) collective-permute-start(bf16[6,64,128]{2,1,0:T(8,128)(2,1)S(1)} %slice.4), channel_id=1, source_target_pairs={{0,1},{4,8},{1,0},{5,9},{2,3},{6,10},{3,2},{7,11},{8,4},{12,16},{9... | collective-permute-start | bytes 294920 | tf_op jit(solution)/shard_map/ppermute | solution.py:513
  8.3 3.4 %inner.1 = (bf16[208,5120]{1,0:T(8,128)(2,1)S(1)}, bf16[208,4608]{1,0:T(8,128)(2,1)S(1)}, bf16[192,4096]{1,0:T(8,128)(2,1)S(1)}, bf16[192,3584]{1,0:T(8,128)(2,1...) custom-call(bf16[32,64,128]{2,1,0:T(8,128)(2,1)S(1)} %get-tuple-elem, ...), custom_call_target="tpu_custom_call" | custom-call | flops 4400000000 | tf_op jit(solution)/shard_map/inner/pallas_call | solution.py:521
  11.7 1.7 %outer.1 = (bf16[192,1024]{1,0:T(8,128)(2,1)S(1)}, bf16[2,64,128]{2,1,0:T(8,128)(2,1)S(1)}, bf16[2,64,128]{2,1,0:T(8,128)(2,1)S(1)}, f32[8,4736]{1,0:T(8,128)S(1)}, f32[8,4736]{1,0:T(8,128)S(1)}) custom-call(bf16[6,64,128]{2,1,0:T(8,128)(2,1)S(1)} %collective-permute-done.1.edges_own, bf16[6,64,128]{2,1,0:T(8,128)(2,1)S(1)} %collective-permute-done.2.edges_other, ...), custom_call_target="tpu_custom_call" | custom-call | flops 2200000000 | tf_op jit(solution)/shard_map/outer/pallas_call | solution.py:544
  13.4 0.1 collective-permute-start.3
  13.5 1.3 %collective-permute-done.3.received = f32[8,4736]{1,0:T(8,128)S(1)} collective-permute-done((f32[8,4736]{1,0:T(8,128)S(1)}, f32[8,4736]{1,0:T(8,128)S(1)}, u32[]{:S(2)}, u32[]{:S(2)}) %collective-permute-start.3) | collective-permute-done | bytes 151584 | tf_op jit(solution)/shard_map/ppermute | solution.py:563
  14.9 2.4 %collective-permute-start.6 = (bf16[8,4736]{1,0:T(8,128)(2,1)S(1)}, bf16[8,4736]{1,0:T(8,128)(2,1)S(1)}, u32[]{:S(2)}, u32[]{:S(2)}) collective-permute-start(bf16[8,4736]{1,0:T(8,128)(2,1)S(1)} %pair.1.held.refs_0_), channel_id=1, source_target_pairs={{0,24},{1,25},{2,26},{3,27},{4,7},{5,6},{6,5},{7,4},{8,16},{9,17},... | collective-permute-start | bytes 227336 | tf_op jit(solution)/shard_map/ppermute | solution.py:570
  17.3 1.1 %collective-permute-start.5 = (bf16[8,4736]{1,0:T(8,128)(2,1)S(1)}, bf16[8,4736]{1,0:T(8,128)(2,1)S(1)}, u32[]{:S(2)}, u32[]{:S(2)}) collective-permute-start(bf16[8,4736]{1,0:T(8,128)(2,1)S(1)} %pair.1.held.refs_0_), channel_id=1, source_target_pairs={{0,16},{1,17},{2,18},{3,19},{4,6},{5,7},{6,4},{7,5},{8,24},{9,25},... | collective-permute-start | bytes 227336 | tf_op jit(solution)/shard_map/ppermute | solution.py:570
  18.5 0.6 %input.1 = (bf16[32,64,128]{2,1,0:T(8,128)(2,1)S(1)}, bf16[32,64,128]{2,1,0:T(8,128)(2,1)S(1)}) custom-call(bf16[8,4736]{1,0:T(8,128)(2,1)S(1)} %pair.1.held.refs_0_, bf16[192,1024]{1,0:T(8,128)(2,1)S(1)} %get-tuple-element.66.e3_b, bf16[192,3584]{1,0:T(8,128)(2,1)S(1)} %get-tuple-element.67.e3, bf16[192,192]{1,0:T(8,128)(2,1)S(1)} %get-tuple-element.68.bwd1, ...), custom_call_target="tpu_custom_call" | custom-call | flops 1100000000 | tf_op jit(solution)/shard_map/input/pallas_call | solution.py:574
  19.1 1.1 %collective-permute-done.6.refs_3_ = bf16[8,4736]{1,0:T(8,128)(2,1)S(1)} collective-permute-done((bf16[8,4736]{1,0:T(8,128)(2,1)S(1)}, bf16[8,4736]{1,0:T(8,128)(2,1)S(1)}, u32[]{:S(2)}, u32[]{:S(2)}) %collective-permute-start.6) | collective-permute-done | bytes 75808 | tf_op jit(solution)/shard_map/ppermute | solution.py:570
  20.2 1.5 %collective-permute-done.5.refs_2_ = bf16[8,4736]{1,0:T(8,128)(2,1)S(1)} collective-permute-done((bf16[8,4736]{1,0:T(8,128)(2,1)S(1)}, bf16[8,4736]{1,0:T(8,128)(2,1)S(1)}, u32[]{:S(2)}, u32[]{:S(2)}) %collective-permute-start.5) | collective-permute-done | bytes 75808 | tf_op jit(solution)/shard_map/ppermute | solution.py:570
  21.7 1.1 %collective-permute-done.4.refs_1_ = bf16[8,4736]{1,0:T(8,128)(2,1)S(1)} collective-permute-done((bf16[8,4736]{1,0:T(8,128)(2,1)S(1)}, bf16[8,4736]{1,0:T(8,128)(2,1)S(1)}, u32[]{:S(2)}, u32[]{:S(2)}) %collective-permute-start.4) | collective-permute-done | bytes 75808 | tf_op jit(solution)/shard_map/ppermute | solution.py:570
  22.8 0.1 collective-permute-start.7
  22.9 3.7 %collective-permute-start.10 = (bf16[8,4736]{1,0:T(8,128)(2,1)S(1)}, bf16[8,4736]{1,0:T(8,128)(2,1)S(1)}, u32[]{:S(2)}, u32[]{:S(2)}) collective-permute-start(bf16[8,4736]{1,0:T(8,128)(2,1)S(1)} %get-tuple-element.79.refs_0_), channel_id=1, source_target_pairs={{0,3},{1,2},{2,1},{3,0},{4,28},{5,29},{6,30},{7,31},{8,11},{9,10},... | collective-permute-start | bytes 227336 | tf_op jit(solution)/shard_map/ppermute | solution.py:570
  26.6 0.8 %collective-permute-start.8 = (bf16[8,4736]{1,0:T(8,128)(2,1)S(1)}, bf16[8,4736]{1,0:T(8,128)(2,1)S(1)}, u32[]{:S(2)}, u32[]{:S(2)}) collective-permute-start(bf16[8,4736]{1,0:T(8,128)(2,1)S(1)} %get-tuple-element.79.refs_0_), channel_id=1, source_target_pairs={{0,1},{1,0},{2,3},{3,2},{4,12},{5,13},{6,14},{7,15},{8,9},{9,8},{1... | collective-permute-start | bytes 227336 | tf_op jit(solution)/shard_map/ppermute | solution.py:570
  27.4 1.3 %outputs.1 = (bf16[1,64,32,128]{3,2,1,0:T(8,128)(2,1)}, bf16[1,64,32,128]{3,2,1,0:T(8,128)(2,1)}, f32[8,128]{1,0:T(8,128)S(1)}) custom-call(bf16[32,64,128]{2,1,0:T(8,128)(2,1)S(1)} %get-tuple-element.73.mine, bf16[32,64,128]{2,1,0:T(8,128)(2,1)S(1)} %collective-permute-done.7.back), custom_call_target="tpu_custom_call" | custom-call | flops 1430000000 | tf_op jit(solution)/shard_map/outputs/pallas_call | solution.py:587
  28.6 0.6 %collective-permute-done.10.refs_3_ = bf16[8,4736]{1,0:T(8,128)(2,1)S(1)} collective-permute-done((bf16[8,4736]{1,0:T(8,128)(2,1)S(1)}, bf16[8,4736]{1,0:T(8,128)(2,1)S(1)}, u32[]{:S(2)}, u32[]{:S(2)}) %collective-permute-start.10) | collective-permute-done | bytes 75808 | tf_op jit(solution)/shard_map/ppermute | solution.py:570
  29.2 2.7 %collective-permute-done.9.refs_2_ = bf16[8,4736]{1,0:T(8,128)(2,1)S(1)} collective-permute-done((bf16[8,4736]{1,0:T(8,128)(2,1)S(1)}, bf16[8,4736]{1,0:T(8,128)(2,1)S(1)}, u32[]{:S(2)}, u32[]{:S(2)}) %collective-permute-start.9) | collective-permute-done | bytes 75808 | tf_op jit(solution)/shard_map/ppermute | solution.py:570
  31.9 0.1 collective-permute-start.11
  32.0 1.4 %collective-permute-done.11.swapped = f32[8,4736]{1,0:T(8,128)S(1)} collective-permute-done((f32[8,4736]{1,0:T(8,128)S(1)}, f32[8,4736]{1,0:T(8,128)S(1)}, u32[]{:S(2)}, u32[]{:S(2)}) %collective-permute-start.11) | collective-permute-done | bytes 151584 | tf_op jit(solution)/shard_map/ppermute | solution.py:600
  33.4 1.0 %grads.1 = (f32[3,3,64,64]{3,2,1,0:T(8,128)}, f32[1,64]{1,0:T(1,128)}, f32[3,3,64,64]{3,2,1,0:T(8,128)}, f32[1,64]{1,0:T(1,128)}) custom-call(f32[8,4736]{1,0:T(8,128)S(1)} %add.3.held, f32[8,4736]{1,0:T(8,128)S(1)} %collective-permute-done.11.swapped), custom_call_target="tpu_custom_call" | custom-call | tf_op jit(solution)/shard_map/grads/pallas_call | solution.py:603
  (11 shorter events, 0.2 us)
Async XLA Ops:
  3.0 3.5 %collective-permute-start = (bf16[38,64,128]{2,1,0:T(8,128)(2,1)S(1)}, bf16[38,64,128]{2,1,0:T(8,128)(2,1)S(1)}, u32[]{:S(2)}, u32[]{:S(2)}) collective-permute-start(bf16[38,64,128]{2,1,0:T(8,128)(2,1)S(1)} %get-tuple-element.45), channel_id=1, source_target_pairs={{0,4},{4,0},{1,5},{5,1},{2,6},{6,2},{3,7},{7,3},{8,12},{12,8},{9,1... | collective-permute-start | bytes 1867784 | tf_op jit(solution)/shard_map/ppermute | solution.py:504
  3.6 8.2 %collective-permute-start.2 = (bf16[6,64,128]{2,1,0:T(8,128)(2,1)S(1)}, bf16[6,64,128]{2,1,0:T(8,128)(2,1)S(1)}, u32[]{:S(2)}, u32[]{:S(2)}) collective-permute-start(bf16[6,64,128]{2,1,0:T(8,128)(2,1)S(1)} %get-tuple-element.46), channel_id=1, source_target_pairs={{0,1},{4,8},{1,0},{5,9},{2,3},{6,10},{3,2},{7,11},{8,4},{12,16},{9... | collective-permute-start | bytes 294920 | tf_op jit(solution)/shard_map/ppermute | solution.py:512
  6.5 5.2 %collective-permute-start.1 = (bf16[6,64,128]{2,1,0:T(8,128)(2,1)S(1)}, bf16[6,64,128]{2,1,0:T(8,128)(2,1)S(1)}, u32[]{:S(2)}, u32[]{:S(2)}) collective-permute-start(bf16[6,64,128]{2,1,0:T(8,128)(2,1)S(1)} %slice.4), channel_id=1, source_target_pairs={{0,1},{4,8},{1,0},{5,9},{2,3},{6,10},{3,2},{7,11},{8,4},{12,16},{9... | collective-permute-start | bytes 294920 | tf_op jit(solution)/shard_map/ppermute | solution.py:513
  13.4 1.4 %collective-permute-start.3 = (f32[8,4736]{1,0:T(8,128)S(1)}, f32[8,4736]{1,0:T(8,128)S(1)}, u32[]{:S(2)}, u32[]{:S(2)}) collective-permute-start(f32[8,4736]{1,0:T(8,128)S(1)} %get-tuple-element.65), channel_id=1, source_target_pairs={{0,4},{4,0},{1,5},{5,1},{2,6},{6,2},{3,7},{7,3},{8,12},{12,8},{9,1... | collective-permute-start | bytes 454664 | tf_op jit(solution)/shard_map/ppermute | solution.py:563
  14.9 5.3 %collective-permute-start.6 = (bf16[8,4736]{1,0:T(8,128)(2,1)S(1)}, bf16[8,4736]{1,0:T(8,128)(2,1)S(1)}, u32[]{:S(2)}, u32[]{:S(2)}) collective-permute-start(bf16[8,4736]{1,0:T(8,128)(2,1)S(1)} %pair.1.held.refs_0_), channel_id=1, source_target_pairs={{0,24},{1,25},{2,26},{3,27},{4,7},{5,6},{6,5},{7,4},{8,16},{9,17},... | collective-permute-start | bytes 227336 | tf_op jit(solution)/shard_map/ppermute | solution.py:570
  17.3 4.4 %collective-permute-start.5 = (bf16[8,4736]{1,0:T(8,128)(2,1)S(1)}, bf16[8,4736]{1,0:T(8,128)(2,1)S(1)}, u32[]{:S(2)}, u32[]{:S(2)}) collective-permute-start(bf16[8,4736]{1,0:T(8,128)(2,1)S(1)} %pair.1.held.refs_0_), channel_id=1, source_target_pairs={{0,16},{1,17},{2,18},{3,19},{4,6},{5,7},{6,4},{7,5},{8,24},{9,25},... | collective-permute-start | bytes 227336 | tf_op jit(solution)/shard_map/ppermute | solution.py:570
  18.4 4.4 %collective-permute-start.4 = (bf16[8,4736]{1,0:T(8,128)(2,1)S(1)}, bf16[8,4736]{1,0:T(8,128)(2,1)S(1)}, u32[]{:S(2)}, u32[]{:S(2)}) collective-permute-start(bf16[8,4736]{1,0:T(8,128)(2,1)S(1)} %pair.1.held.refs_0_), channel_id=1, source_target_pairs={{0,8},{1,9},{2,10},{3,11},{4,5},{5,4},{6,7},{7,6},{8,0},{9,1},{10,... | collective-permute-start | bytes 227336 | tf_op jit(solution)/shard_map/ppermute | solution.py:570
  22.8 4.5 %collective-permute-start.7 = (bf16[32,64,128]{2,1,0:T(8,128)(2,1)S(1)}, bf16[32,64,128]{2,1,0:T(8,128)(2,1)S(1)}, u32[]{:S(2)}, u32[]{:S(2)}) collective-permute-start(bf16[32,64,128]{2,1,0:T(8,128)(2,1)S(1)} %get-tuple-element.75), channel_id=1, source_target_pairs={{0,4},{4,0},{1,5},{5,1},{2,6},{6,2},{3,7},{7,3},{8,12},{12,8},{9,1... | collective-permute-start | bytes 1572872 | tf_op jit(solution)/shard_map/ppermute | solution.py:586
  22.9 6.3 %collective-permute-start.10 = (bf16[8,4736]{1,0:T(8,128)(2,1)S(1)}, bf16[8,4736]{1,0:T(8,128)(2,1)S(1)}, u32[]{:S(2)}, u32[]{:S(2)}) collective-permute-start(bf16[8,4736]{1,0:T(8,128)(2,1)S(1)} %get-tuple-element.79.refs_0_), channel_id=1, source_target_pairs={{0,3},{1,2},{2,1},{3,0},{4,28},{5,29},{6,30},{7,31},{8,11},{9,10},... | collective-permute-start | bytes 227336 | tf_op jit(solution)/shard_map/ppermute | solution.py:570
  26.6 5.3 %collective-permute-start.9 = (bf16[8,4736]{1,0:T(8,128)(2,1)S(1)}, bf16[8,4736]{1,0:T(8,128)(2,1)S(1)}, u32[]{:S(2)}, u32[]{:S(2)}) collective-permute-start(bf16[8,4736]{1,0:T(8,128)(2,1)S(1)} %get-tuple-element.79.refs_0_), channel_id=1, source_target_pairs={{0,2},{1,3},{2,0},{3,1},{4,20},{5,21},{6,22},{7,23},{8,10},{9,11},... | collective-permute-start | bytes 227336 | tf_op jit(solution)/shard_map/ppermute | solution.py:570
  26.6 5.3 %collective-permute-start.8 = (bf16[8,4736]{1,0:T(8,128)(2,1)S(1)}, bf16[8,4736]{1,0:T(8,128)(2,1)S(1)}, u32[]{:S(2)}, u32[]{:S(2)}) collective-permute-start(bf16[8,4736]{1,0:T(8,128)(2,1)S(1)} %get-tuple-element.79.refs_0_), channel_id=1, source_target_pairs={{0,1},{1,0},{2,3},{3,2},{4,12},{5,13},{6,14},{7,15},{8,9},{9,8},{1... | collective-permute-start | bytes 227336 | tf_op jit(solution)/shard_map/ppermute | solution.py:570
  31.9 1.4 %collective-permute-start.11 = (f32[8,4736]{1,0:T(8,128)S(1)}, f32[8,4736]{1,0:T(8,128)S(1)}, u32[]{:S(2)}, u32[]{:S(2)}) collective-permute-start(f32[8,4736]{1,0:T(8,128)S(1)} %add.3.held), channel_id=1, source_target_pairs={{0,4},{4,0},{1,5},{5,1},{2,6},{6,2},{3,7},{7,3},{8,12},{12,8},{9,1... | collective-permute-start | bytes 454664 | tf_op jit(solution)/shard_map/ppermute | solution.py:600

commit v2 on v1

--- a/solution.py
+++ b/solution.py
@@ -13,6 +13,15 @@
 SWAP = [(0, 1), (1, 0)]
 CONTRACT = (((1,), (1,)), ((), ()))
 TILES = 37
+
+
+def half_of(side, place, plane):
+    bits = place ^ plane
+    return (side ^ bits ^ (bits >> 1) ^ (bits >> 2) ^ (bits >> 3)) & 1
+
+
+def own_half():
+    return half_of(lax.axis_index("sx"), lax.axis_index("sy"), lax.axis_index("grp"))
 
 
 def shape_of(shape, dtype):
@@ -52,7 +61,6 @@
     b2_v,
     image_v,
     cot_v,
-    wides,
     sems,
 ):
     side = lax.axis_index("sx")
@@ -70,13 +78,11 @@
         copy = pltpu.make_async_copy(src, dst, sems.at[len(jobs) + n])
         copy.start()
         small.append(copy)
-    for n, (copy, chans, dst, out) in enumerate(jobs):
+    for copy, chans, dst, out in jobs:
         copy.wait()
-        wide = wides.at[n]
-        wide[...] = dst[chans].astype(F32).reshape(wide.shape)
+        block = jnp.transpose(dst[chans], (1, 0, 2))
         for h in range(rows):
-            row = wide[pl.ds(h, 16, stride=rows), :]
-            out[turned(side, h, rows), chans, :] = row.astype(BF16)
+            out[turned(side, h, rows), chans, :] = block[h]
     swap[0 : half + 4] = image_p[half - 4 : rows]
     for k in range(half + 2):
         swap[half + 4 + k] = cot_p[rows - 1 - k]
@@ -298,10 +304,10 @@
     def keep(value):
         return jnp.where(outside, 0.0, value.astype(F32)).astype(BF16)
 
-    for half_of, edges in ((side, edges_own), (other, edges_other)):
-        image_s[half_of] = keep(edges[0:4])
-        cot_s[half_of, 0] = keep(edges[5])
-        cot_s[half_of, 1] = keep(edges[4])
+    for cols, edges in ((side, edges_own), (other, edges_other)):
+        image_s[cols] = keep(edges[0:4])
+        cot_s[cols, 0] = keep(edges[5])
+        cot_s[cols, 1] = keep(edges[4])
     cot_s[side, 2:4] = cot_p[0:2]
     cot_s[other, 2:4] = swapped[half + 4 : half + 6]
     ones = jnp.ones((16, x3_b.shape[1]), BF16)
@@ -366,11 +372,12 @@
         for t in range(72)
     ]
     empty = jnp.zeros((8, 128), F32)
+    own = own_half()
     low, high = tiles[:36] + [biases], tiles[36:] + [empty]
     for t in range(TILES):
         at = slice(128 * t, 128 * t + 128)
-        grads_own[:, at] = jnp.where(side == 0, low[t], high[t])
-        grads_send[:, at] = jnp.where(side == 0, high[t], low[t])
+        grads_own[:, at] = jnp.where(own == 0, low[t], high[t])
+        grads_send[:, at] = jnp.where(own == 0, high[t], low[t])
 
 
 def pair_kernel(own, received, out):
@@ -421,11 +428,11 @@
 
 
 def grads_kernel(held, swapped, gw1, gb1, gw2, gb2):
-    side = lax.axis_index("sx")
+    own = own_half()
 
     def tile(part, t):
         at = slice(128 * t, 128 * t + 128)
-        return jnp.where(side == part, held[:, at], swapped[:, at])
+        return jnp.where(own == part, held[:, at], swapped[:, at])
 
     for block in range(24):
         part, first = block // 12, 3 * (block % 12)
@@ -452,11 +459,14 @@
         for k in range(3):
             pairs = []
             for s in range(places):
-                for x, (axis, masks) in enumerate(plan):
+                for x in range(2):
                     for g in range(planes):
+                        part = half_of(x, s, g)
+                        axis, masks = plan[part]
                         if k < len(masks):
                             t, h = (s ^ masks[k], g) if axis == 0 else (s, g ^ masks[k])
-                            pairs.append(((2 * s + x) * planes + g, (2 * t + x) * planes + h))
+                            y = half_of(part, t, h)
+                            pairs.append(((2 * s + x) * planes + g, (2 * t + y) * planes + h))
             if pairs:
                 stage.append(pairs)
         stages.append(stage)
@@ -493,7 +503,6 @@
         scratch_shapes=[
             pltpu.VMEM((chans, rows, cols), BF16),
             pltpu.VMEM((chans, rows, cols), BF16),
-            pltpu.VMEM((chans // 8, 16 * rows, cols), F32),
             pltpu.SemaphoreType.DMA((chans // 8 + 4,)),
         ],
         name="pack",

time: 34.5 us -> 32.8 us (0.951)
  waiting for transfers between devices: 9.63 us -> 8.12 us
  Pallas kernels: 10.8 us -> 9.95 us
  starting transfers between devices: 13.1 us -> 13.9 us
    ppermute x6, waiting for transfers between devices: 6.92 us -> 5.51 us  [local(): received = [lax.ppermute(held, axes, pairs) for pairs in stage]]
    ppermute x1, starting transfers between devices: 0.07 us -> 1.32 us  [local(): back = lax.ppermute(theirs, 'sx', SWAP)]
    pallas_call x1, Pallas kernels: 2.41 us -> 1.53 us  [local(): call(pack_kernel, out_shape=[rows_of(rows), rows_of(rows), rows_of(2 * ha...]
    ppermute x6, starting transfers between devices: 8 us -> 7.38 us  [local(): received = [lax.ppermute(held, axes, pairs) for pairs in stage]]
  transfers between devices with their start and end apart: 12 -> 12, of which waited for: 7 -> 7; matrix products, arithmetic and copies ran while one was open for 0% -> 0% of each run, Pallas kernels for 16% -> 17%
where the time goes in v2:
time: 32.8 us; the launch traced here: 32.7 us
  starting transfers between devices  13.9 us (42%)
  Pallas kernels  9.95 us (30%)
  waiting for transfers between devices  8.12 us (25%)
  between operations  0.72 us (2%)
    ppermute x6, starting transfers between devices, local(): received = [lax.ppermute(held, axes, pairs) for pairs in stage]  7.38 us
    ppermute x6, waiting for transfers between devices, local(): received = [lax.ppermute(held, axes, pairs) for pairs in stage]  5.51 us
    pallas_call x1, Pallas kernels, local(): call(inner_kernel, out_shape=[flat(208, half + 4), flat(208, half + 2), f...  3.44 us
    ppermute x1, starting transfers between devices, local(): edges_other = lax.ppermute(edges, axes, across)  2.65 us
    ppermute x1, starting transfers between devices, local(): edges_own = lax.ppermute(swapped[half:half + 6], axes, across)  1.72 us
    pallas_call x1, Pallas kernels, local(): call(outer_kernel, out_shape=[flat(192, 4), rows_of(2), rows_of(2), half_...  1.69 us
    pallas_call x1, Pallas kernels, local(): call(pack_kernel, out_shape=[rows_of(rows), rows_of(rows), rows_of(2 * ha...  1.53 us
    ppermute x1, waiting for transfers between devices, local(): grads_received = lax.ppermute(grads_send, 'sx', SWAP)  1.33 us
  transfers between devices with their start and end apart: 12, of which 7 were waited for; matrix products, arithmetic and copies ran while one was open for 0% of the time, Pallas kernels for 17%

profile of v2, /device:TPU:0, one launch (start us, length us, event | category | flops | bytes accessed | tf_op | source)
XLA Modules:
  0.0 32.7 jit_solution(12195691978617261260)
XLA Ops:
  0.6 1.5 %pack.1 = (bf16[32,64,128]{2,1,0:T(8,128)(2,1)S(1)}, bf16[32,64,128]{2,1,0:T(8,128)(2,1)S(1)}, bf16[38,64,128]{2,1,0:T(8,128)(2,1)S(1)}, bf16[6,64,128]{2,1,0:T(...) custom-call(bf16[1,64,32,128]{3,2,1,0:T(8,128)(2,1)} %image_ref.1, ...), custom_call_target="tpu_custom_call" | custom-call | tf_op jit(solution)/shard_map/pack/pallas_call | solution.py:490
  2.2 0.5 %collective-permute-start = (bf16[38,64,128]{2,1,0:T(8,128)(2,1)S(1)}, bf16[38,64,128]{2,1,0:T(8,128)(2,1)S(1)}, u32[]{:S(2)}, u32[]{:S(2)}) collective-permute-start(bf16[38,64,128]{2,1,0:T(8,128)(2,1)S(1)} %get-tuple-element.45), channel_id=1, source_target_pairs={{0,4},{4,0},{1,5},{5,1},{2,6},{6,2},{3,7},{7,3},{8,12},{12,8},{9,1... | collective-permute-start | bytes 1867784 | tf_op jit(solution)/shard_map/ppermute | solution.py:513
  2.7 2.6 %collective-permute-start.2 = (bf16[6,64,128]{2,1,0:T(8,128)(2,1)S(1)}, bf16[6,64,128]{2,1,0:T(8,128)(2,1)S(1)}, u32[]{:S(2)}, u32[]{:S(2)}) collective-permute-start(bf16[6,64,128]{2,1,0:T(8,128)(2,1)S(1)} %get-tuple-element.46), channel_id=1, source_target_pairs={{0,1},{4,8},{1,0},{5,9},{2,3},{6,10},{3,2},{7,11},{8,4},{12,16},{9... | collective-permute-start | bytes 294920 | tf_op jit(solution)/shard_map/ppermute | solution.py:521
  5.3 0.3 weights.1
  5.7 1.7 %collective-permute-start.1 = (bf16[6,64,128]{2,1,0:T(8,128)(2,1)S(1)}, bf16[6,64,128]{2,1,0:T(8,128)(2,1)S(1)}, u32[]{:S(2)}, u32[]{:S(2)}) collective-permute-start(bf16[6,64,128]{2,1,0:T(8,128)(2,1)S(1)} %slice.4), channel_id=1, source_target_pairs={{0,1},{4,8},{1,0},{5,9},{2,3},{6,10},{3,2},{7,11},{8,4},{12,16},{9... | collective-permute-start | bytes 294920 | tf_op jit(solution)/shard_map/ppermute | solution.py:522
  7.4 3.4 %inner.1 = (bf16[208,5120]{1,0:T(8,128)(2,1)S(1)}, bf16[208,4608]{1,0:T(8,128)(2,1)S(1)}, bf16[192,4096]{1,0:T(8,128)(2,1)S(1)}, bf16[192,3584]{1,0:T(8,128)(2,1...) custom-call(bf16[32,64,128]{2,1,0:T(8,128)(2,1)S(1)} %get-tuple-elem, ...), custom_call_target="tpu_custom_call" | custom-call | flops 4400000000 | tf_op jit(solution)/shard_map/inner/pallas_call | solution.py:530
  10.9 1.7 %outer.1 = (bf16[192,1024]{1,0:T(8,128)(2,1)S(1)}, bf16[2,64,128]{2,1,0:T(8,128)(2,1)S(1)}, bf16[2,64,128]{2,1,0:T(8,128)(2,1)S(1)}, f32[8,4736]{1,0:T(8,128)S(1)}, f32[8,4736]{1,0:T(8,128)S(1)}) custom-call(bf16[6,64,128]{2,1,0:T(8,128)(2,1)S(1)} %collective-permute-done.1.edges_own, bf16[6,64,128]{2,1,0:T(8,128)(2,1)S(1)} %collective-permute-done.2.edges_other, ...), custom_call_target="tpu_custom_call" | custom-call | flops 2200000000 | tf_op jit(solution)/shard_map/outer/pallas_call | solution.py:553
  12.6 0.1 collective-permute-start.3
  12.7 1.3 %collective-permute-done.3.received = f32[8,4736]{1,0:T(8,128)S(1)} collective-permute-done((f32[8,4736]{1,0:T(8,128)S(1)}, f32[8,4736]{1,0:T(8,128)S(1)}, u32[]{:S(2)}, u32[]{:S(2)}) %collective-permute-start.3) | collective-permute-done | bytes 151584 | tf_op jit(solution)/shard_map/ppermute | solution.py:572
  14.0 2.4 %collective-permute-start.6 = (bf16[8,4736]{1,0:T(8,128)(2,1)S(1)}, bf16[8,4736]{1,0:T(8,128)(2,1)S(1)}, u32[]{:S(2)}, u32[]{:S(2)}) collective-permute-start(bf16[8,4736]{1,0:T(8,128)(2,1)S(1)} %pair.1.held.refs_0_), channel_id=1, source_target_pairs={{0,24},{1,2},{2,1},{3,27},{4,7},{5,29},{6,30},{7,4},{8,11},{9,17},... | collective-permute-start | bytes 227336 | tf_op jit(solution)/shard_map/ppermute | solution.py:579
  16.5 0.8 %collective-permute-start.5 = (bf16[8,4736]{1,0:T(8,128)(2,1)S(1)}, bf16[8,4736]{1,0:T(8,128)(2,1)S(1)}, u32[]{:S(2)}, u32[]{:S(2)}) collective-permute-start(bf16[8,4736]{1,0:T(8,128)(2,1)S(1)} %pair.1.held.refs_0_), channel_id=1, source_target_pairs={{0,20},{1,7},{2,4},{3,23},{4,2},{5,17},{6,18},{7,1},{8,14},{9,29},... | collective-permute-start | bytes 227336 | tf_op jit(solution)/shard_map/ppermute | solution.py:579
  17.3 0.6 %input.1 = (bf16[32,64,128]{2,1,0:T(8,128)(2,1)S(1)}, bf16[32,64,128]{2,1,0:T(8,128)(2,1)S(1)}) custom-call(bf16[8,4736]{1,0:T(8,128)(2,1)S(1)} %pair.1.held.refs_0_, bf16[192,1024]{1,0:T(8,128)(2,1)S(1)} %get-tuple-element.66.e3_b, bf16[192,3584]{1,0:T(8,128)(2,1)S(1)} %get-tuple-element.67.e3, bf16[192,192]{1,0:T(8,128)(2,1)S(1)} %get-tuple-element.68.bwd1, ...), custom_call_target="tpu_custom_call" | custom-call | flops 1100000000 | tf_op jit(solution)/shard_map/input/pallas_call | solution.py:583
  18.0 1.4 %collective-permute-done.6.refs_3_ = bf16[8,4736]{1,0:T(8,128)(2,1)S(1)} collective-permute-done((bf16[8,4736]{1,0:T(8,128)(2,1)S(1)}, bf16[8,4736]{1,0:T(8,128)(2,1)S(1)}, u32[]{:S(2)}, u32[]{:S(2)}) %collective-permute-start.6) | collective-permute-done | bytes 75808 | tf_op jit(solution)/shard_map/ppermute | solution.py:579
  19.4 0.9 %collective-permute-done.5.refs_2_ = bf16[8,4736]{1,0:T(8,128)(2,1)S(1)} collective-permute-done((bf16[8,4736]{1,0:T(8,128)(2,1)S(1)}, bf16[8,4736]{1,0:T(8,128)(2,1)S(1)}, u32[]{:S(2)}, u32[]{:S(2)}) %collective-permute-start.5) | collective-permute-done | bytes 75808 | tf_op jit(solution)/shard_map/ppermute | solution.py:579
  20.3 0.8 %collective-permute-done.4.refs_1_ = bf16[8,4736]{1,0:T(8,128)(2,1)S(1)} collective-permute-done((bf16[8,4736]{1,0:T(8,128)(2,1)S(1)}, bf16[8,4736]{1,0:T(8,128)(2,1)S(1)}, u32[]{:S(2)}, u32[]{:S(2)}) %collective-permute-start.4) | collective-permute-done | bytes 75808 | tf_op jit(solution)/shard_map/ppermute | solution.py:579
  21.1 1.3 %collective-permute-start.7 = (bf16[32,64,128]{2,1,0:T(8,128)(2,1)S(1)}, bf16[32,64,128]{2,1,0:T(8,128)(2,1)S(1)}, u32[]{:S(2)}, u32[]{:S(2)}) collective-permute-start(bf16[32,64,128]{2,1,0:T(8,128)(2,1)S(1)} %get-tuple-element.75), channel_id=1, source_target_pairs={{0,4},{4,0},{1,5},{5,1},{2,6},{6,2},{3,7},{7,3},{8,12},{12,8},{9,1... | collective-permute-start | bytes 1572872 | tf_op jit(solution)/shard_map/ppermute | solution.py:595
  22.4 2.4 %collective-permute-start.10 = (bf16[8,4736]{1,0:T(8,128)(2,1)S(1)}, bf16[8,4736]{1,0:T(8,128)(2,1)S(1)}, u32[]{:S(2)}, u32[]{:S(2)}) collective-permute-start(bf16[8,4736]{1,0:T(8,128)(2,1)S(1)} %get-tuple-element.79.refs_0_), channel_id=1, source_target_pairs={{0,3},{1,25},{2,26},{3,0},{4,28},{5,6},{6,5},{7,31},{8,16},{9,10},... | collective-permute-start | bytes 227336 | tf_op jit(solution)/shard_map/ppermute | solution.py:579
  24.8 1.7 %collective-permute-start.8 = (bf16[8,4736]{1,0:T(8,128)(2,1)S(1)}, bf16[8,4736]{1,0:T(8,128)(2,1)S(1)}, u32[]{:S(2)}, u32[]{:S(2)}) collective-permute-start(bf16[8,4736]{1,0:T(8,128)(2,1)S(1)} %get-tuple-element.79.refs_0_), channel_id=1, source_target_pairs={{0,5},{1,13},{2,14},{3,6},{4,8},{5,0},{6,3},{7,11},{8,4},{9,12},{1... | collective-permute-start | bytes 227336 | tf_op jit(solution)/shard_map/ppermute | solution.py:579
  26.5 1.3 %outputs.1 = (bf16[1,64,32,128]{3,2,1,0:T(8,128)(2,1)}, bf16[1,64,32,128]{3,2,1,0:T(8,128)(2,1)}, f32[8,128]{1,0:T(8,128)S(1)}) custom-call(bf16[32,64,128]{2,1,0:T(8,128)(2,1)S(1)} %get-tuple-element.73.mine, bf16[32,64,128]{2,1,0:T(8,128)(2,1)S(1)} %collective-permute-done.7.back), custom_call_target="tpu_custom_call" | custom-call | flops 1430000000 | tf_op jit(solution)/shard_map/outputs/pallas_call | solution.py:596
  27.8 0.9 %collective-permute-done.10.refs_3_ = bf16[8,4736]{1,0:T(8,128)(2,1)S(1)} collective-permute-done((bf16[8,4736]{1,0:T(8,128)(2,1)S(1)}, bf16[8,4736]{1,0:T(8,128)(2,1)S(1)}, u32[]{:S(2)}, u32[]{:S(2)}) %collective-permute-start.10) | collective-permute-done | bytes 75808 | tf_op jit(solution)/shard_map/ppermute | solution.py:579
  28.7 1.5 %collective-permute-done.9.refs_2_ = bf16[8,4736]{1,0:T(8,128)(2,1)S(1)} collective-permute-done((bf16[8,4736]{1,0:T(8,128)(2,1)S(1)}, bf16[8,4736]{1,0:T(8,128)(2,1)S(1)}, u32[]{:S(2)}, u32[]{:S(2)}) %collective-permute-start.9) | collective-permute-done | bytes 75808 | tf_op jit(solution)/shard_map/ppermute | solution.py:579
  30.3 0.2 collective-permute-start.11
  30.4 1.3 %collective-permute-done.11.swapped = f32[8,4736]{1,0:T(8,128)S(1)} collective-permute-done((f32[8,4736]{1,0:T(8,128)S(1)}, f32[8,4736]{1,0:T(8,128)S(1)}, u32[]{:S(2)}, u32[]{:S(2)}) %collective-permute-start.11) | collective-permute-done | bytes 151584 | tf_op jit(solution)/shard_map/ppermute | solution.py:609
  31.7 1.0 %grads.1 = (f32[3,3,64,64]{3,2,1,0:T(8,128)}, f32[1,64]{1,0:T(1,128)}, f32[3,3,64,64]{3,2,1,0:T(8,128)}, f32[1,64]{1,0:T(1,128)}) custom-call(f32[8,4736]{1,0:T(8,128)S(1)} %add.3.held, f32[8,4736]{1,0:T(8,128)S(1)} %collective-permute-done.11.swapped), custom_call_target="tpu_custom_call" | custom-call | tf_op jit(solution)/shard_map/grads/pallas_call | solution.py:612
  (11 shorter events, 0.2 us)
Async XLA Ops:
  2.2 3.5 %collective-permute-start = (bf16[38,64,128]{2,1,0:T(8,128)(2,1)S(1)}, bf16[38,64,128]{2,1,0:T(8,128)(2,1)S(1)}, u32[]{:S(2)}, u32[]{:S(2)}) collective-permute-start(bf16[38,64,128]{2,1,0:T(8,128)(2,1)S(1)} %get-tuple-element.45), channel_id=1, source_target_pairs={{0,4},{4,0},{1,5},{5,1},{2,6},{6,2},{3,7},{7,3},{8,12},{12,8},{9,1... | collective-permute-start | bytes 1867784 | tf_op jit(solution)/shard_map/ppermute | solution.py:513
  2.7 8.2 %collective-permute-start.2 = (bf16[6,64,128]{2,1,0:T(8,128)(2,1)S(1)}, bf16[6,64,128]{2,1,0:T(8,128)(2,1)S(1)}, u32[]{:S(2)}, u32[]{:S(2)}) collective-permute-start(bf16[6,64,128]{2,1,0:T(8,128)(2,1)S(1)} %get-tuple-element.46), channel_id=1, source_target_pairs={{0,1},{4,8},{1,0},{5,9},{2,3},{6,10},{3,2},{7,11},{8,4},{12,16},{9... | collective-permute-start | bytes 294920 | tf_op jit(solution)/shard_map/ppermute | solution.py:521
  5.7 5.2 %collective-permute-start.1 = (bf16[6,64,128]{2,1,0:T(8,128)(2,1)S(1)}, bf16[6,64,128]{2,1,0:T(8,128)(2,1)S(1)}, u32[]{:S(2)}, u32[]{:S(2)}) collective-permute-start(bf16[6,64,128]{2,1,0:T(8,128)(2,1)S(1)} %slice.4), channel_id=1, source_target_pairs={{0,1},{4,8},{1,0},{5,9},{2,3},{6,10},{3,2},{7,11},{8,4},{12,16},{9... | collective-permute-start | bytes 294920 | tf_op jit(solution)/shard_map/ppermute | solution.py:522
  12.6 1.4 %collective-permute-start.3 = (f32[8,4736]{1,0:T(8,128)S(1)}, f32[8,4736]{1,0:T(8,128)S(1)}, u32[]{:S(2)}, u32[]{:S(2)}) collective-permute-start(f32[8,4736]{1,0:T(8,128)S(1)} %get-tuple-element.65), channel_id=1, source_target_pairs={{0,4},{4,0},{1,5},{5,1},{2,6},{6,2},{3,7},{7,3},{8,12},{12,8},{9,1... | collective-permute-start | bytes 454664 | tf_op jit(solution)/shard_map/ppermute | solution.py:572
  14.0 5.3 %collective-permute-start.6 = (bf16[8,4736]{1,0:T(8,128)(2,1)S(1)}, bf16[8,4736]{1,0:T(8,128)(2,1)S(1)}, u32[]{:S(2)}, u32[]{:S(2)}) collective-permute-start(bf16[8,4736]{1,0:T(8,128)(2,1)S(1)} %pair.1.held.refs_0_), channel_id=1, source_target_pairs={{0,24},{1,2},{2,1},{3,27},{4,7},{5,29},{6,30},{7,4},{8,11},{9,17},... | collective-permute-start | bytes 227336 | tf_op jit(solution)/shard_map/ppermute | solution.py:579
  16.5 3.8 %collective-permute-start.5 = (bf16[8,4736]{1,0:T(8,128)(2,1)S(1)}, bf16[8,4736]{1,0:T(8,128)(2,1)S(1)}, u32[]{:S(2)}, u32[]{:S(2)}) collective-permute-start(bf16[8,4736]{1,0:T(8,128)(2,1)S(1)} %pair.1.held.refs_0_), channel_id=1, source_target_pairs={{0,20},{1,7},{2,4},{3,23},{4,2},{5,17},{6,18},{7,1},{8,14},{9,29},... | collective-permute-start | bytes 227336 | tf_op jit(solution)/shard_map/ppermute | solution.py:579
  17.2 3.8 %collective-permute-start.4 = (bf16[8,4736]{1,0:T(8,128)(2,1)S(1)}, bf16[8,4736]{1,0:T(8,128)(2,1)S(1)}, u32[]{:S(2)}, u32[]{:S(2)}) collective-permute-start(bf16[8,4736]{1,0:T(8,128)(2,1)S(1)} %pair.1.held.refs_0_), channel_id=1, source_target_pairs={{0,12},{1,4},{2,7},{3,15},{4,1},{5,9},{6,10},{7,2},{8,13},{9,5},{1... | collective-permute-start | bytes 227336 | tf_op jit(solution)/shard_map/ppermute | solution.py:579
  21.1 5.4 %collective-permute-start.7 = (bf16[32,64,128]{2,1,0:T(8,128)(2,1)S(1)}, bf16[32,64,128]{2,1,0:T(8,128)(2,1)S(1)}, u32[]{:S(2)}, u32[]{:S(2)}) collective-permute-start(bf16[32,64,128]{2,1,0:T(8,128)(2,1)S(1)} %get-tuple-element.75), channel_id=1, source_target_pairs={{0,4},{4,0},{1,5},{5,1},{2,6},{6,2},{3,7},{7,3},{8,12},{12,8},{9,1... | collective-permute-start | bytes 1572872 | tf_op jit(solution)/shard_map/ppermute | solution.py:595
  22.4 6.3 %collective-permute-start.10 = (bf16[8,4736]{1,0:T(8,128)(2,1)S(1)}, bf16[8,4736]{1,0:T(8,128)(2,1)S(1)}, u32[]{:S(2)}, u32[]{:S(2)}) collective-permute-start(bf16[8,4736]{1,0:T(8,128)(2,1)S(1)} %get-tuple-element.79.refs_0_), channel_id=1, source_target_pairs={{0,3},{1,25},{2,26},{3,0},{4,28},{5,6},{6,5},{7,31},{8,16},{9,10},... | collective-permute-start | bytes 227336 | tf_op jit(solution)/shard_map/ppermute | solution.py:579
  24.8 5.4 %collective-permute-start.9 = (bf16[8,4736]{1,0:T(8,128)(2,1)S(1)}, bf16[8,4736]{1,0:T(8,128)(2,1)S(1)}, u32[]{:S(2)}, u32[]{:S(2)}) collective-permute-start(bf16[8,4736]{1,0:T(8,128)(2,1)S(1)} %get-tuple-element.79.refs_0_), channel_id=1, source_target_pairs={{0,6},{1,21},{2,22},{3,5},{4,16},{5,3},{6,0},{7,19},{8,28},{9,15},... | collective-permute-start | bytes 227336 | tf_op jit(solution)/shard_map/ppermute | solution.py:579
  24.8 5.4 %collective-permute-start.8 = (bf16[8,4736]{1,0:T(8,128)(2,1)S(1)}, bf16[8,4736]{1,0:T(8,128)(2,1)S(1)}, u32[]{:S(2)}, u32[]{:S(2)}) collective-permute-start(bf16[8,4736]{1,0:T(8,128)(2,1)S(1)} %get-tuple-element.79.refs_0_), channel_id=1, source_target_pairs={{0,5},{1,13},{2,14},{3,6},{4,8},{5,0},{6,3},{7,11},{8,4},{9,12},{1... | collective-permute-start | bytes 227336 | tf_op jit(solution)/shard_map/ppermute | solution.py:579
  30.3 1.4 %collective-permute-start.11 = (f32[8,4736]{1,0:T(8,128)S(1)}, f32[8,4736]{1,0:T(8,128)S(1)}, u32[]{:S(2)}, u32[]{:S(2)}) collective-permute-start(f32[8,4736]{1,0:T(8,128)S(1)} %add.3.held), channel_id=1, source_target_pairs={{0,4},{4,0},{1,5},{5,1},{2,6},{6,2},{3,7},{7,3},{8,12},{12,8},{9,1... | collective-permute-start | bytes 454664 | tf_op jit(solution)/shard_map/ppermute | solution.py:609

commit v3 on v2

--- a/solution.py
+++ b/solution.py
@@ -380,7 +380,7 @@
         grads_send[:, at] = jnp.where(own == 0, high[t], low[t])
 
 
-def pair_kernel(own, received, out):
+def pair_kernel(passed, own, received, out, through):
     out[...] = (own[...] + received[...]).astype(BF16)
 
 
@@ -392,15 +392,11 @@
     out[...] = (terms[0] * factor).astype(out.dtype)
 
 
-def passing_add(add, passed, *refs):
-    add(*refs[:-1])
-
-
 def behind_add(add, done, *refs):
     add(*refs)
 
 
-def input_kernel(held, e3_b, e3, bwd1, mine_a, mine_b, theirs_a, theirs_b, mine, theirs):
+def input_kernel(e3_b, e3, bwd1, mine_a, mine_b, theirs_a, theirs_b, mine, theirs):
     side = lax.axis_index("sx")
     half = mine.shape[0] // 2
     width = 2 * mine.shape[2]
@@ -570,42 +566,37 @@
         *near(x3, h3, d3, slopes, grad2, grad1),
     )
     grads_received = lax.ppermute(grads_send, "sx", SWAP)
-    held = call(pair_kernel, out_shape=pltpu.VMEM((8, TILES * 128), BF16), name="pair")(
-        *near(grads_own, grads_received)
-    )
+    mine, theirs = call(
+        input_kernel,
+        out_shape=[rows_of(rows), rows_of(rows)],
+        cost_estimate=lasting(0.7),
+        name="input",
+    )(*near(e3_b, e3, bwd1, mine_a, mine_b, theirs_a, theirs_b))
+    held, theirs = call(
+        pair_kernel,
+        out_shape=[pltpu.VMEM((8, TILES * 128), BF16), rows_of(rows)],
+        input_output_aliases={0: 1},
+        name="pair",
+    )(*near(theirs, grads_own, grads_received))
+    back = lax.ppermute(theirs, "sx", SWAP)
+    out, image_grad, done = call(
+        outputs_kernel,
+        out_shape=[shape_of(image.shape, BF16)] * 2 + [pltpu.VMEM((8, 128), F32)],
+        scratch_shapes=[pltpu.VMEM((2, rows, chans, cols), BF16)],
+        cost_estimate=lasting(1.3),
+        name="outputs",
+    )(*near(mine, back))
     stages = exchange_stages(places, planes)
     for n, stage in enumerate(stages):
         final = n == len(stages) - 1
         received = [lax.ppermute(held, axes, pairs) for pairs in stage]
-        sums = pltpu.VMEM((8, TILES * 128), F32 if final else BF16)
         add = functools.partial(add_kernel, factor if final else 1.0)
-        if n == 0:
-            mine, theirs = call(
-                input_kernel,
-                out_shape=[rows_of(rows), rows_of(rows)],
-                cost_estimate=lasting(1.0),
-                name="input",
-            )(*near(held, e3_b, e3, bwd1, mine_a, mine_b, theirs_a, theirs_b))
-            held, theirs = call(
-                functools.partial(passing_add, add),
-                out_shape=[sums, rows_of(rows)],
-                input_output_aliases={0: 1},
-                name="add",
-            )(*near(theirs, held, *received))
-            back = lax.ppermute(theirs, "sx", SWAP)
-            out, image_grad, done = call(
-                outputs_kernel,
-                out_shape=[shape_of(image.shape, BF16)] * 2 + [pltpu.VMEM((8, 128), F32)],
-                scratch_shapes=[pltpu.VMEM((2, rows, chans, cols), BF16)],
-                cost_estimate=lasting(1.3),
-                name="outputs",
-            )(*near(mine, back))
-        elif n == 1:
-            held = call(functools.partial(behind_add, add), out_shape=sums, name="add")(
-                *near(done, held, *received)
-            )
-        else:
-            held = call(add, out_shape=sums, name="add")(*near(held, *received))
+        behind = [done] if n == 0 else []
+        held = call(
+            functools.partial(behind_add, add) if behind else add,
+            out_shape=pltpu.VMEM((8, TILES * 128), F32 if final else BF16),
+            name="add",
+        )(*near(*behind, held, *received))
     swapped_sums = lax.ppermute(held, "sx", SWAP)
     weight_shape = shape_of((3, 3, chans, chans), F32)
     bias_shape = shape_of((1, chans), F32)

time: 32.8 us -> 32.5 us (level)
  starting transfers between devices: 13.9 us -> 13 us
  waiting for transfers between devices: 8.12 us -> 8.79 us
    ppermute x6, waiting for transfers between devices: 5.51 us -> 7.02 us  [local(): received = [lax.ppermute(held, axes, pairs) for pairs in stage]]
    ppermute x1, starting transfers between devices: 1.32 us -> 0.21 us  [local(): back = lax.ppermute(theirs, 'sx', SWAP)]
    ppermute x1, waiting for transfers between devices: 1.33 us -> 0.68 us  [local(): grads_received = lax.ppermute(grads_send, 'sx', SWAP)]
where the time goes in v3:
time: 32.5 us; the launch traced here: 32.4 us
  starting transfers between devices  13 us (40%)
  Pallas kernels  9.92 us (31%)
  waiting for transfers between devices  8.79 us (27%)
  between operations  0.72 us (2%)
    ppermute x6, starting transfers between devices, local(): received = [lax.ppermute(held, axes, pairs) for pairs in stage]  7.38 us
    ppermute x6, waiting for transfers between devices, local(): received = [lax.ppermute(held, axes, pairs) for pairs in stage]  7.02 us
    pallas_call x1, Pallas kernels, local(): call(inner_kernel, out_shape=[flat(208, half + 4), flat(208, half + 2), f...  3.44 us
    ppermute x1, starting transfers between devices, local(): edges_other = lax.ppermute(edges, axes, across)  2.65 us
    ppermute x1, starting transfers between devices, local(): edges_own = lax.ppermute(swapped[half:half + 6], axes, across)  1.72 us
    pallas_call x1, Pallas kernels, local(): call(outer_kernel, out_shape=[flat(192, 4), rows_of(2), rows_of(2), half_...  1.69 us
    pallas_call x1, Pallas kernels, local(): call(pack_kernel, out_shape=[rows_of(rows), rows_of(rows), rows_of(2 * ha...  1.53 us
    pallas_call x1, Pallas kernels, local(): call(outputs_kernel, out_shape=[shape_of(image.shape, BF16)] * 2 + [pltpu...  1.26 us
  transfers between devices with their start and end apart: 12, of which 7 were waited for; matrix products, arithmetic and copies ran while one was open for 0% of the time, Pallas kernels for 17%

profile of v3, /device:TPU:0, one launch (start us, length us, event | category | flops | bytes accessed | tf_op | source)
XLA Modules:
  0.0 32.4 jit_solution(11030305408781093543)
XLA Ops:
  0.6 1.5 %pack.1 = (bf16[32,64,128]{2,1,0:T(8,128)(2,1)S(1)}, bf16[32,64,128]{2,1,0:T(8,128)(2,1)S(1)}, bf16[38,64,128]{2,1,0:T(8,128)(2,1)S(1)}, bf16[6,64,128]{2,1,0:T(...) custom-call(bf16[1,64,32,128]{3,2,1,0:T(8,128)(2,1)} %image_ref.1, ...), custom_call_target="tpu_custom_call" | custom-call | tf_op jit(solution)/shard_map/pack/pallas_call | solution.py:486
  2.2 0.5 %collective-permute-start = (bf16[38,64,128]{2,1,0:T(8,128)(2,1)S(1)}, bf16[38,64,128]{2,1,0:T(8,128)(2,1)S(1)}, u32[]{:S(2)}, u32[]{:S(2)}) collective-permute-start(bf16[38,64,128]{2,1,0:T(8,128)(2,1)S(1)} %get-tuple-element.45), channel_id=1, source_target_pairs={{0,4},{4,0},{1,5},{5,1},{2,6},{6,2},{3,7},{7,3},{8,12},{12,8},{9,1... | collective-permute-start | bytes 1867784 | tf_op jit(solution)/shard_map/ppermute | solution.py:509
  2.7 2.6 %collective-permute-start.2 = (bf16[6,64,128]{2,1,0:T(8,128)(2,1)S(1)}, bf16[6,64,128]{2,1,0:T(8,128)(2,1)S(1)}, u32[]{:S(2)}, u32[]{:S(2)}) collective-permute-start(bf16[6,64,128]{2,1,0:T(8,128)(2,1)S(1)} %get-tuple-element.46), channel_id=1, source_target_pairs={{0,1},{4,8},{1,0},{5,9},{2,3},{6,10},{3,2},{7,11},{8,4},{12,16},{9... | collective-permute-start | bytes 294920 | tf_op jit(solution)/shard_map/ppermute | solution.py:517
  5.3 0.3 weights.1
  5.7 1.7 %collective-permute-start.1 = (bf16[6,64,128]{2,1,0:T(8,128)(2,1)S(1)}, bf16[6,64,128]{2,1,0:T(8,128)(2,1)S(1)}, u32[]{:S(2)}, u32[]{:S(2)}) collective-permute-start(bf16[6,64,128]{2,1,0:T(8,128)(2,1)S(1)} %slice.4), channel_id=1, source_target_pairs={{0,1},{4,8},{1,0},{5,9},{2,3},{6,10},{3,2},{7,11},{8,4},{12,16},{9... | collective-permute-start | bytes 294920 | tf_op jit(solution)/shard_map/ppermute | solution.py:518
  7.4 3.4 %inner.1 = (bf16[208,5120]{1,0:T(8,128)(2,1)S(1)}, bf16[208,4608]{1,0:T(8,128)(2,1)S(1)}, bf16[192,4096]{1,0:T(8,128)(2,1)S(1)}, bf16[192,3584]{1,0:T(8,128)(2,1...) custom-call(bf16[32,64,128]{2,1,0:T(8,128)(2,1)S(1)} %get-tuple-elem, ...), custom_call_target="tpu_custom_call" | custom-call | flops 4400000000 | tf_op jit(solution)/shard_map/inner/pallas_call | solution.py:526
  10.9 1.7 %outer.1 = (bf16[192,1024]{1,0:T(8,128)(2,1)S(1)}, bf16[2,64,128]{2,1,0:T(8,128)(2,1)S(1)}, bf16[2,64,128]{2,1,0:T(8,128)(2,1)S(1)}, f32[8,4736]{1,0:T(8,128)S(1)}, f32[8,4736]{1,0:T(8,128)S(1)}) custom-call(bf16[6,64,128]{2,1,0:T(8,128)(2,1)S(1)} %collective-permute-done.1.edges_own, bf16[6,64,128]{2,1,0:T(8,128)(2,1)S(1)} %collective-permute-done.2.edges_other, ...), custom_call_target="tpu_custom_call" | custom-call | flops 2200000000 | tf_op jit(solution)/shard_map/outer/pallas_call | solution.py:549
  12.6 0.1 collective-permute-start.3
  12.7 0.6 %input.1 = (bf16[32,64,128]{2,1,0:T(8,128)(2,1)S(1)}, bf16[32,64,128]{2,1,0:T(8,128)(2,1)S(1)}) custom-call(bf16[192,1024]{1,0:T(8,128)(2,1)S(1)} %get-tuple-element.64.e3_b, bf16[192,3584]{1,0:T(8,128)(2,1)S(1)} %get-tuple-element.65.e3, bf16[192,192]{1,0:T(8,128)(2,1)S(1)} %get-tuple-element.66.bwd1, bf16[14,64,128]{2,1,0:T(8,128)(2,1)S(1)} %get-tuple-element.67.mine_a, ...), custom_call_target="tpu_custom_call" | custom-call | flops 770000000 | tf_op jit(solution)/shard_map/input/pallas_call | solution.py:569
  13.3 0.7 %collective-permute-done.3.received = f32[8,4736]{1,0:T(8,128)S(1)} collective-permute-done((f32[8,4736]{1,0:T(8,128)S(1)}, f32[8,4736]{1,0:T(8,128)S(1)}, u32[]{:S(2)}, u32[]{:S(2)}) %collective-permute-start.3) | collective-permute-done | bytes 151584 | tf_op jit(solution)/shard_map/ppermute | solution.py:568
  14.0 0.2 collective-permute-start.4
  14.2 2.4 %collective-permute-start.7 = (bf16[8,4736]{1,0:T(8,128)(2,1)S(1)}, bf16[8,4736]{1,0:T(8,128)(2,1)S(1)}, u32[]{:S(2)}, u32[]{:S(2)}) collective-permute-start(bf16[8,4736]{1,0:T(8,128)(2,1)S(1)} %get-tuple-element.79.refs_0_), channel_id=1, source_target_pairs={{0,24},{1,2},{2,1},{3,27},{4,7},{5,29},{6,30},{7,4},{8,11},{9,17},... | collective-permute-start | bytes 227336 | tf_op jit(solution)/shard_map/ppermute | solution.py:592
  16.6 0.8 %collective-permute-start.6 = (bf16[8,4736]{1,0:T(8,128)(2,1)S(1)}, bf16[8,4736]{1,0:T(8,128)(2,1)S(1)}, u32[]{:S(2)}, u32[]{:S(2)}) collective-permute-start(bf16[8,4736]{1,0:T(8,128)(2,1)S(1)} %get-tuple-element.79.refs_0_), channel_id=1, source_target_pairs={{0,20},{1,7},{2,4},{3,23},{4,2},{5,17},{6,18},{7,1},{8,14},{9,29},... | collective-permute-start | bytes 227336 | tf_op jit(solution)/shard_map/ppermute | solution.py:592
  17.4 1.3 %outputs.1 = (bf16[1,64,32,128]{3,2,1,0:T(8,128)(2,1)}, bf16[1,64,32,128]{3,2,1,0:T(8,128)(2,1)}, f32[8,128]{1,0:T(8,128)S(1)}) custom-call(bf16[32,64,128]{2,1,0:T(8,128)(2,1)S(1)} %get-tuple-element.71.mine, bf16[32,64,128]{2,1,0:T(8,128)(2,1)S(1)} %collective-permute-done.4.back), custom_call_target="tpu_custom_call" | custom-call | flops 1430000000 | tf_op jit(solution)/shard_map/outputs/pallas_call | solution.py:582
  18.7 0.8 %collective-permute-done.7.refs_3_ = bf16[8,4736]{1,0:T(8,128)(2,1)S(1)} collective-permute-done((bf16[8,4736]{1,0:T(8,128)(2,1)S(1)}, bf16[8,4736]{1,0:T(8,128)(2,1)S(1)}, u32[]{:S(2)}, u32[]{:S(2)}) %collective-permute-start.7) | collective-permute-done | bytes 75808 | tf_op jit(solution)/shard_map/ppermute | solution.py:592
  19.5 0.9 %collective-permute-done.6.refs_2_ = bf16[8,4736]{1,0:T(8,128)(2,1)S(1)} collective-permute-done((bf16[8,4736]{1,0:T(8,128)(2,1)S(1)}, bf16[8,4736]{1,0:T(8,128)(2,1)S(1)}, u32[]{:S(2)}, u32[]{:S(2)}) %collective-permute-start.6) | collective-permute-done | bytes 75808 | tf_op jit(solution)/shard_map/ppermute | solution.py:592
  20.4 0.8 %collective-permute-done.5.refs_1_ = bf16[8,4736]{1,0:T(8,128)(2,1)S(1)} collective-permute-done((bf16[8,4736]{1,0:T(8,128)(2,1)S(1)}, bf16[8,4736]{1,0:T(8,128)(2,1)S(1)}, u32[]{:S(2)}, u32[]{:S(2)}) %collective-permute-start.5) | collective-permute-done | bytes 75808 | tf_op jit(solution)/shard_map/ppermute | solution.py:592
  21.2 3.7 %collective-permute-start.10 = (bf16[8,4736]{1,0:T(8,128)(2,1)S(1)}, bf16[8,4736]{1,0:T(8,128)(2,1)S(1)}, u32[]{:S(2)}, u32[]{:S(2)}) collective-permute-start(bf16[8,4736]{1,0:T(8,128)(2,1)S(1)} %add.2.refs_0_), channel_id=1, source_target_pairs={{0,3},{1,25},{2,26},{3,0},{4,28},{5,6},{6,5},{7,31},{8,16},{9,10},... | collective-permute-start | bytes 227336 | tf_op jit(solution)/shard_map/ppermute | solution.py:592
  24.9 0.5 %collective-permute-start.8 = (bf16[8,4736]{1,0:T(8,128)(2,1)S(1)}, bf16[8,4736]{1,0:T(8,128)(2,1)S(1)}, u32[]{:S(2)}, u32[]{:S(2)}) collective-permute-start(bf16[8,4736]{1,0:T(8,128)(2,1)S(1)} %add.2.refs_0_), channel_id=1, source_target_pairs={{0,5},{1,13},{2,14},{3,6},{4,8},{5,0},{6,3},{7,11},{8,4},{9,12},{1... | collective-permute-start | bytes 227336 | tf_op jit(solution)/shard_map/ppermute | solution.py:592
  25.4 2.1 %collective-permute-done.10.refs_3_ = bf16[8,4736]{1,0:T(8,128)(2,1)S(1)} collective-permute-done((bf16[8,4736]{1,0:T(8,128)(2,1)S(1)}, bf16[8,4736]{1,0:T(8,128)(2,1)S(1)}, u32[]{:S(2)}, u32[]{:S(2)}) %collective-permute-start.10) | collective-permute-done | bytes 75808 | tf_op jit(solution)/shard_map/ppermute | solution.py:592
  27.5 2.5 %collective-permute-done.9.refs_2_ = bf16[8,4736]{1,0:T(8,128)(2,1)S(1)} collective-permute-done((bf16[8,4736]{1,0:T(8,128)(2,1)S(1)}, bf16[8,4736]{1,0:T(8,128)(2,1)S(1)}, u32[]{:S(2)}, u32[]{:S(2)}) %collective-permute-start.9) | collective-permute-done | bytes 75808 | tf_op jit(solution)/shard_map/ppermute | solution.py:592
  30.0 0.4 %collective-permute-start.11 = (f32[8,4736]{1,0:T(8,128)S(1)}, f32[8,4736]{1,0:T(8,128)S(1)}, u32[]{:S(2)}, u32[]{:S(2)}) collective-permute-start(f32[8,4736]{1,0:T(8,128)S(1)} %add.3.held), channel_id=1, source_target_pairs={{0,4},{4,0},{1,5},{5,1},{2,6},{6,2},{3,7},{7,3},{8,12},{12,8},{9,1... | collective-permute-start | bytes 454664 | tf_op jit(solution)/shard_map/ppermute | solution.py:600
  30.3 1.1 %collective-permute-done.11.swapped = f32[8,4736]{1,0:T(8,128)S(1)} collective-permute-done((f32[8,4736]{1,0:T(8,128)S(1)}, f32[8,4736]{1,0:T(8,128)S(1)}, u32[]{:S(2)}, u32[]{:S(2)}) %collective-permute-start.11) | collective-permute-done | bytes 151584 | tf_op jit(solution)/shard_map/ppermute | solution.py:600
  31.4 1.0 %grads.1 = (f32[3,3,64,64]{3,2,1,0:T(8,128)}, f32[1,64]{1,0:T(1,128)}, f32[3,3,64,64]{3,2,1,0:T(8,128)}, f32[1,64]{1,0:T(1,128)}) custom-call(f32[8,4736]{1,0:T(8,128)S(1)} %add.3.held, f32[8,4736]{1,0:T(8,128)S(1)} %collective-permute-done.11.swapped), custom_call_target="tpu_custom_call" | custom-call | tf_op jit(solution)/shard_map/grads/pallas_call | solution.py:603
  (11 shorter events, 0.2 us)
Async XLA Ops:
  2.2 3.5 %collective-permute-start = (bf16[38,64,128]{2,1,0:T(8,128)(2,1)S(1)}, bf16[38,64,128]{2,1,0:T(8,128)(2,1)S(1)}, u32[]{:S(2)}, u32[]{:S(2)}) collective-permute-start(bf16[38,64,128]{2,1,0:T(8,128)(2,1)S(1)} %get-tuple-element.45), channel_id=1, source_target_pairs={{0,4},{4,0},{1,5},{5,1},{2,6},{6,2},{3,7},{7,3},{8,12},{12,8},{9,1... | collective-permute-start | bytes 1867784 | tf_op jit(solution)/shard_map/ppermute | solution.py:509
  2.7 8.1 %collective-permute-start.2 = (bf16[6,64,128]{2,1,0:T(8,128)(2,1)S(1)}, bf16[6,64,128]{2,1,0:T(8,128)(2,1)S(1)}, u32[]{:S(2)}, u32[]{:S(2)}) collective-permute-start(bf16[6,64,128]{2,1,0:T(8,128)(2,1)S(1)} %get-tuple-element.46), channel_id=1, source_target_pairs={{0,1},{4,8},{1,0},{5,9},{2,3},{6,10},{3,2},{7,11},{8,4},{12,16},{9... | collective-permute-start | bytes 294920 | tf_op jit(solution)/shard_map/ppermute | solution.py:517
  5.7 5.2 %collective-permute-start.1 = (bf16[6,64,128]{2,1,0:T(8,128)(2,1)S(1)}, bf16[6,64,128]{2,1,0:T(8,128)(2,1)S(1)}, u32[]{:S(2)}, u32[]{:S(2)}) collective-permute-start(bf16[6,64,128]{2,1,0:T(8,128)(2,1)S(1)} %slice.4), channel_id=1, source_target_pairs={{0,1},{4,8},{1,0},{5,9},{2,3},{6,10},{3,2},{7,11},{8,4},{12,16},{9... | collective-permute-start | bytes 294920 | tf_op jit(solution)/shard_map/ppermute | solution.py:518
  12.6 1.4 %collective-permute-start.3 = (f32[8,4736]{1,0:T(8,128)S(1)}, f32[8,4736]{1,0:T(8,128)S(1)}, u32[]{:S(2)}, u32[]{:S(2)}) collective-permute-start(f32[8,4736]{1,0:T(8,128)S(1)} %get-tuple-element.74), channel_id=1, source_target_pairs={{0,4},{4,0},{1,5},{5,1},{2,6},{6,2},{3,7},{7,3},{8,12},{12,8},{9,1... | collective-permute-start | bytes 454664 | tf_op jit(solution)/shard_map/ppermute | solution.py:568
  14.0 3.4 %collective-permute-start.4 = (bf16[32,64,128]{2,1,0:T(8,128)(2,1)S(1)}, bf16[32,64,128]{2,1,0:T(8,128)(2,1)S(1)}, u32[]{:S(2)}, u32[]{:S(2)}) collective-permute-start(bf16[32,64,128]{2,1,0:T(8,128)(2,1)S(1)} %get-tuple-element.75), channel_id=1, source_target_pairs={{0,4},{4,0},{1,5},{5,1},{2,6},{6,2},{3,7},{7,3},{8,12},{12,8},{9,1... | collective-permute-start | bytes 1572872 | tf_op jit(solution)/shard_map/ppermute | solution.py:581
  14.2 5.3 %collective-permute-start.7 = (bf16[8,4736]{1,0:T(8,128)(2,1)S(1)}, bf16[8,4736]{1,0:T(8,128)(2,1)S(1)}, u32[]{:S(2)}, u32[]{:S(2)}) collective-permute-start(bf16[8,4736]{1,0:T(8,128)(2,1)S(1)} %get-tuple-element.79.refs_0_), channel_id=1, source_target_pairs={{0,24},{1,2},{2,1},{3,27},{4,7},{5,29},{6,30},{7,4},{8,11},{9,17},... | collective-permute-start | bytes 227336 | tf_op jit(solution)/shard_map/ppermute | solution.py:592
  16.6 3.8 %collective-permute-start.6 = (bf16[8,4736]{1,0:T(8,128)(2,1)S(1)}, bf16[8,4736]{1,0:T(8,128)(2,1)S(1)}, u32[]{:S(2)}, u32[]{:S(2)}) collective-permute-start(bf16[8,4736]{1,0:T(8,128)(2,1)S(1)} %get-tuple-element.79.refs_0_), channel_id=1, source_target_pairs={{0,20},{1,7},{2,4},{3,23},{4,2},{5,17},{6,18},{7,1},{8,14},{9,29},... | collective-permute-start | bytes 227336 | tf_op jit(solution)/shard_map/ppermute | solution.py:592
  17.4 3.8 %collective-permute-start.5 = (bf16[8,4736]{1,0:T(8,128)(2,1)S(1)}, bf16[8,4736]{1,0:T(8,128)(2,1)S(1)}, u32[]{:S(2)}, u32[]{:S(2)}) collective-permute-start(bf16[8,4736]{1,0:T(8,128)(2,1)S(1)} %get-tuple-element.79.refs_0_), channel_id=1, source_target_pairs={{0,12},{1,4},{2,7},{3,15},{4,1},{5,9},{6,10},{7,2},{8,13},{9,5},{1... | collective-permute-start | bytes 227336 | tf_op jit(solution)/shard_map/ppermute | solution.py:592
  21.2 6.2 %collective-permute-start.10 = (bf16[8,4736]{1,0:T(8,128)(2,1)S(1)}, bf16[8,4736]{1,0:T(8,128)(2,1)S(1)}, u32[]{:S(2)}, u32[]{:S(2)}) collective-permute-start(bf16[8,4736]{1,0:T(8,128)(2,1)S(1)} %add.2.refs_0_), channel_id=1, source_target_pairs={{0,3},{1,25},{2,26},{3,0},{4,28},{5,6},{6,5},{7,31},{8,16},{9,10},... | collective-permute-start | bytes 227336 | tf_op jit(solution)/shard_map/ppermute | solution.py:592
  24.9 5.0 %collective-permute-start.9 = (bf16[8,4736]{1,0:T(8,128)(2,1)S(1)}, bf16[8,4736]{1,0:T(8,128)(2,1)S(1)}, u32[]{:S(2)}, u32[]{:S(2)}) collective-permute-start(bf16[8,4736]{1,0:T(8,128)(2,1)S(1)} %add.2.refs_0_), channel_id=1, source_target_pairs={{0,6},{1,21},{2,22},{3,5},{4,16},{5,3},{6,0},{7,19},{8,28},{9,15},... | collective-permute-start | bytes 227336 | tf_op jit(solution)/shard_map/ppermute | solution.py:592
  24.9 5.0 %collective-permute-start.8 = (bf16[8,4736]{1,0:T(8,128)(2,1)S(1)}, bf16[8,4736]{1,0:T(8,128)(2,1)S(1)}, u32[]{:S(2)}, u32[]{:S(2)}) collective-permute-start(bf16[8,4736]{1,0:T(8,128)(2,1)S(1)} %add.2.refs_0_), channel_id=1, source_target_pairs={{0,5},{1,13},{2,14},{3,6},{4,8},{5,0},{6,3},{7,11},{8,4},{9,12},{1... | collective-permute-start | bytes 227336 | tf_op jit(solution)/shard_map/ppermute | solution.py:592
  30.0 1.4 %collective-permute-start.11 = (f32[8,4736]{1,0:T(8,128)S(1)}, f32[8,4736]{1,0:T(8,128)S(1)}, u32[]{:S(2)}, u32[]{:S(2)}) collective-permute-start(f32[8,4736]{1,0:T(8,128)S(1)} %add.3.held), channel_id=1, source_target_pairs={{0,4},{4,0},{1,5},{5,1},{2,6},{6,2},{3,7},{7,3},{8,12},{12,8},{9,1... | collective-permute-start | bytes 454664 | tf_op jit(solution)/shard_map/ppermute | solution.py:600

commit v4 on v3

--- a/solution.py
+++ b/solution.py
@@ -42,6 +42,24 @@
 
 def turned(side, index, count):
     return index + side * (count - 1 - 2 * index)
+
+
+def cut_edges(image_p, cot_p, edges):
+    for k in range(4):
+        edges[k] = image_p[3 - k]
+    edges[4:6] = cot_p[0:2]
+
+
+def repack_kernel(image, cot, image_p, cot_p, edges):
+    side = lax.axis_index("sx")
+    rows = image.shape[2]
+    for src, out in ((image, image_p), (cot, cot_p)):
+        for c in range(image.shape[1] // 16):
+            chans = slice(16 * c, 16 * c + 16)
+            block = jnp.transpose(src[0, chans], (1, 0, 2))
+            for h in range(rows):
+                out[turned(side, h, rows), chans, :] = block[h]
+    cut_edges(image_p, cot_p, edges)
 
 
 def pack_kernel(
@@ -53,7 +71,6 @@
     b2,
     image_p,
     cot_p,
-    swap,
     edges,
     w1_v,
     b1_v,
@@ -65,7 +82,6 @@
 ):
     side = lax.axis_index("sx")
     rows = image_ref.shape[2]
-    half = rows // 2
     jobs, small = [], []
     sources = ((image_ref, image_v, image_p), (cot_ref, cot_v, cot_p))
     for c in range(image_ref.shape[1] // 16):
@@ -83,12 +99,7 @@
         block = jnp.transpose(dst[chans], (1, 0, 2))
         for h in range(rows):
             out[turned(side, h, rows), chans, :] = block[h]
-    swap[0 : half + 4] = image_p[half - 4 : rows]
-    for k in range(half + 2):
-        swap[half + 4 + k] = cot_p[rows - 1 - k]
-    for k in range(4):
-        edges[k] = image_p[3 - k]
-    edges[4:6] = cot_p[0:2]
+    cut_edges(image_p, cot_p, edges)
     for copy in small:
         copy.wait()
 
@@ -187,7 +198,8 @@
 def inner_kernel(
     image_p,
     cot_p,
-    swapped,
+    image_o,
+    cot_o,
     fwd1,
     fwd2,
     bwd2,
@@ -214,9 +226,8 @@
     other = 1 - side
     image_s[side] = image_p[0 : half + 4]
     cot_s[side] = cot_p[0 : half + 2]
-    for p in range(half + 4):
-        image_s[other, p] = swapped[half + 3 - p]
-    cot_s[other] = swapped[half + 4 : 2 * half + 6]
+    image_s[other] = image_o[0 : half + 4]
+    cot_s[other] = cot_o[0 : half + 2]
     ones = jnp.ones((16, x3.shape[1]), BF16)
     x3[192:208, :] = ones
     h3[192:208, :] = ones[:, : h3.shape[1]]
@@ -267,7 +278,7 @@
     edges_own,
     edges_other,
     cot_p,
-    swapped,
+    cot_o,
     fwd1,
     fwd2,
     bwd2,
@@ -309,7 +320,7 @@
         cot_s[cols, 0] = keep(edges[5])
         cot_s[cols, 1] = keep(edges[4])
     cot_s[side, 2:4] = cot_p[0:2]
-    cot_s[other, 2:4] = swapped[half + 4 : half + 6]
+    cot_s[other, 2:4] = cot_o[0:2]
     ones = jnp.ones((16, x3_b.shape[1]), BF16)
     x3_b[192:208, :] = ones
     h3_b[192:208, :] = ones
@@ -483,12 +494,13 @@
     def flat(height, count):
         return pltpu.VMEM((height, count * width), BF16)
 
-    image_p, cot_p, swap, edges, w1, b1, w2, b2 = call(
+    image_o = lax.ppermute(image, "sx", SWAP)
+    cot_o = lax.ppermute(cotangent, "sx", SWAP)
+    image_p, cot_p, edges, w1, b1, w2, b2 = call(
         pack_kernel,
         out_shape=[
             rows_of(rows),
             rows_of(rows),
-            rows_of(2 * half + 6),
             rows_of(6),
             pltpu.VMEM(weight_one.shape, BF16),
             pltpu.VMEM((1, chans), F32),
@@ -501,12 +513,18 @@
             pltpu.VMEM((chans, rows, cols), BF16),
             pltpu.SemaphoreType.DMA((chans // 8 + 4,)),
         ],
+        cost_estimate=lasting(1.5),
         name="pack",
     )(
         *far(image, cotangent, weight_one, bias_one.reshape(1, chans)),
         *far(weight_two, bias_two.reshape(1, chans)),
     )
-    swapped = lax.ppermute(swap, "sx", SWAP)
+    image_o, cot_o, edges_next = call(
+        repack_kernel,
+        out_shape=[rows_of(rows), rows_of(rows), rows_of(6)],
+        cost_estimate=lasting(0.5),
+        name="repack",
+    )(*near(image_o, cot_o))
     across = []
     for s in range(places):
         for g in range(planes):
@@ -515,7 +533,7 @@
             across.append((upper, upper + planes if s < places - 1 else upper ^ 1))
     axes = ("sy", "sx", "grp")
     edges_other = lax.ppermute(edges, axes, across)
-    edges_own = lax.ppermute(swapped[half : half + 6], axes, across)
+    edges_own = lax.ppermute(edges_next, axes, across)
     fwd1, fwd2, bwd2, bwd1, bias1, bias2 = call(
         weights_kernel,
         out_shape=[pltpu.VMEM((192, 192), BF16)] * 4 + [pltpu.VMEM((64, 128), F32)] * 2,
@@ -544,7 +562,7 @@
         ],
         cost_estimate=lasting(4.0),
         name="inner",
-    )(*near(image_p, cot_p, swapped, fwd1, fwd2, bwd2, bias1, bias2))
+    )(*near(image_p, cot_p, image_o, cot_o, fwd1, fwd2, bwd2, bias1, bias2))
     half_grads = pltpu.VMEM((8, TILES * 128), F32)
     e3_b, mine_b, theirs_b, grads_own, grads_send = call(
         outer_kernel,
@@ -562,7 +580,7 @@
         cost_estimate=lasting(2.0),
         name="outer",
     )(
-        *near(edges_own, edges_other, cot_p, swapped, fwd1, fwd2, bwd2, bias1, bias2),
+        *near(edges_own, edges_other, cot_p, cot_o, fwd1, fwd2, bwd2, bias1, bias2),
         *near(x3, h3, d3, slopes, grad2, grad1),
     )
     grads_received = lax.ppermute(grads_send, "sx", SWAP)

time: 32.5 us -> 33 us (1.015)
  waiting for transfers between devices: 8.79 us -> 9.31 us
  starting transfers between devices: 13 us -> 12.5 us
  Pallas kernels: 9.92 us -> 10.3 us
    ppermute x2 -> x3, starting transfers between devices: 2.24 us -> 1.14 us  [the longest x1 0.55 us: local(): edges_own = lax.ppermute(edges_next, axes, across)]
    ppermute x2 -> x3, waiting for transfers between devices: 0.01 us -> 0.67 us  [the longest x1 0.66 us: local(): edges_own = lax.ppermute(edges_next, axes, across)]
    ppermute x1, starting transfers between devices: 2.65 us -> 3.07 us  [local(): edges_other = lax.ppermute(edges, axes, across)]
    pallas_call x1 -> x2, Pallas kernels: 1.53 us -> 1.87 us  [the longest x1 1.48 us: local(): call(pack_kernel, out_shape=[rows_of(rows), rows_of(rows), rows_of(6), pl...]
  transfers between devices with their start and end apart: 12 -> 13, of which waited for: 7 -> 8; matrix products, arithmetic and copies ran while one was open for 0% -> 0% of each run, Pallas kernels for 17% -> 23%
where the time goes in v4:
time: 33 us; the launch traced here: 32.8 us
  starting transfers between devices  12.5 us (38%)
  Pallas kernels  10.3 us (31%)
  waiting for transfers between devices  9.31 us (28%)
  between operations  0.72 us (2%)
    ppermute x6, starting transfers between devices, local(): received = [lax.ppermute(held, axes, pairs) for pairs in stage]  7.41 us
    ppermute x6, waiting for transfers between devices, local(): received = [lax.ppermute(held, axes, pairs) for pairs in stage]  7.05 us
    pallas_call x1, Pallas kernels, local(): call(inner_kernel, out_shape=[flat(208, half + 4), flat(208, half + 2), f...  3.46 us
    ppermute x1, starting transfers between devices, local(): edges_other = lax.ppermute(edges, axes, across)  3.07 us
    pallas_call x1, Pallas kernels, local(): call(outer_kernel, out_shape=[flat(192, 4), rows_of(2), rows_of(2), half_...  1.68 us
    pallas_call x1, Pallas kernels, local(): call(pack_kernel, out_shape=[rows_of(rows), rows_of(rows), rows_of(6), pl...  1.48 us
    pallas_call x1, Pallas kernels, local(): call(outputs_kernel, out_shape=[shape_of(image.shape, BF16)] * 2 + [pltpu...  1.26 us
    ppermute x1, waiting for transfers between devices, local(): swapped_sums = lax.ppermute(held, 'sx', SWAP)  1.08 us
  transfers between devices with their start and end apart: 13, of which 8 were waited for; matrix products, arithmetic and copies ran while one was open for 0% of the time, Pallas kernels for 23%

profile of v4, /device:TPU:0, one launch (start us, length us, event | category | flops | bytes accessed | tf_op | source)
XLA Modules:
  0.0 32.8 jit_solution(5043528160355347964)
XLA Ops:
  0.6 0.5 %collective-permute-start = (bf16[1,64,32,128]{3,2,1,0:T(8,128)(2,1)}, bf16[1,64,32,128]{3,2,1,0:T(8,128)(2,1)S(1)}, u32[]{:S(2)}, u32[]{:S(2)}) collective-permute-start(bf16[1,64,32,128]{3,2,1,0:T(8,128)(2,1)} %image_ref.1), channel_id=1, source_target_pairs={{0,4},{4,0},{1,5},{5,1},{2,6},{6,2},{3,7},{7,3},{8,12},{12,8},{9,1... | collective-permute-start | bytes 1572872 | tf_op jit(solution)/shard_map/ppermute | solution.py:497
  1.2 1.5 %pack.1 = (bf16[32,64,128]{2,1,0:T(8,128)(2,1)S(1)}, bf16[32,64,128]{2,1,0:T(8,128)(2,1)S(1)}, bf16[6,64,128]{2,1,0:T(8,128)(2,1)S(1)}, bf16[3,3,64,64]{3,2,1,0:...) custom-call(bf16[1,64,32,128]{3,2,1,0:T(8,128)(2,1)} %image_ref.1, ...), custom_call_target="tpu_custom_call" | custom-call | flops 1650000000 | tf_op jit(solution)/shard_map/pack/pallas_call | solution.py:499
  2.7 3.1 %collective-permute-start.3 = (bf16[6,64,128]{2,1,0:T(8,128)(2,1)S(1)}, bf16[6,64,128]{2,1,0:T(8,128)(2,1)S(1)}, u32[]{:S(2)}, u32[]{:S(2)}) collective-permute-start(bf16[6,64,128]{2,1,0:T(8,128)(2,1)S(1)} %get-tuple-element.48), channel_id=1, source_target_pairs={{0,1},{4,8},{1,0},{5,9},{2,3},{6,10},{3,2},{7,11},{8,4},{12,16},{9... | collective-permute-start | bytes 294920 | tf_op jit(solution)/shard_map/ppermute | solution.py:535
  5.8 0.3 weights.1
  6.1 0.4 %repack.1 = (bf16[32,64,128]{2,1,0:T(8,128)(2,1)S(1)}, bf16[32,64,128]{2,1,0:T(8,128)(2,1)S(1)}, bf16[6,64,128]{2,1,0:T(8,128)(2,1)S(1)}) custom-call(bf16[1,64,32,128]{3,2,1,0:T(8,128)(2,1)S(1)} %collective-permute-done.image, bf16[1,64,32,128]{3,2,1,0:T(8,128)(2,1)S(1)} %collective-permute-done.1.cot), custom_call_target="tpu_custom_call" | custom-call | flops 550000000 | tf_op jit(solution)/shard_map/repack/pallas_call | solution.py:522
  6.5 0.5 %collective-permute-start.2 = (bf16[6,64,128]{2,1,0:T(8,128)(2,1)S(1)}, bf16[6,64,128]{2,1,0:T(8,128)(2,1)S(1)}, u32[]{:S(2)}, u32[]{:S(2)}) collective-permute-start(bf16[6,64,128]{2,1,0:T(8,128)(2,1)S(1)} %get-tuple-element.47), channel_id=1, source_target_pairs={{0,1},{4,8},{1,0},{5,9},{2,3},{6,10},{3,2},{7,11},{8,4},{12,16},{9... | collective-permute-start | bytes 294920 | tf_op jit(solution)/shard_map/ppermute | solution.py:536
  7.0 3.5 %inner.1 = (bf16[208,5120]{1,0:T(8,128)(2,1)S(1)}, bf16[208,4608]{1,0:T(8,128)(2,1)S(1)}, bf16[192,4096]{1,0:T(8,128)(2,1)S(1)}, bf16[192,3584]{1,0:T(8,128)(2,1...) custom-call(bf16[32,64,128]{2,1,0:T(8,128)(2,1)S(1)} %get-tuple-elem, ...), custom_call_target="tpu_custom_call" | custom-call | flops 4400000000 | tf_op jit(solution)/shard_map/inner/pallas_call | solution.py:544
  10.5 0.7 %collective-permute-done.2.edges_own = bf16[6,64,128]{2,1,0:T(8,128)(2,1)S(1)} collective-permute-done((bf16[6,64,128]{2,1,0:T(8,128)(2,1)S(1)}, bf16[6,64,128]{2,1,0:T(8,128)(2,1)S(1)}, u32[]{:S(2)}, u32[]{:S(2)}) %collective-permute-start.2) | collective-permute-done | bytes 98336 | tf_op jit(solution)/shard_map/ppermute | solution.py:536
  11.2 1.7 %outer.1 = (bf16[192,1024]{1,0:T(8,128)(2,1)S(1)}, bf16[2,64,128]{2,1,0:T(8,128)(2,1)S(1)}, bf16[2,64,128]{2,1,0:T(8,128)(2,1)S(1)}, f32[8,4736]{1,0:T(8,128)S(1)}, f32[8,4736]{1,0:T(8,128)S(1)}) custom-call(bf16[6,64,128]{2,1,0:T(8,128)(2,1)S(1)} %collective-permute-done.2.edges_own, bf16[6,64,128]{2,1,0:T(8,128)(2,1)S(1)} %collective-permute-done.3.edges_other, ...), custom_call_target="tpu_custom_call" | custom-call | flops 2200000000 | tf_op jit(solution)/shard_map/outer/pallas_call | solution.py:567
  13.2 0.6 %input.1 = (bf16[32,64,128]{2,1,0:T(8,128)(2,1)S(1)}, bf16[32,64,128]{2,1,0:T(8,128)(2,1)S(1)}) custom-call(bf16[192,1024]{1,0:T(8,128)(2,1)S(1)} %get-tuple-element.68.e3_b, bf16[192,3584]{1,0:T(8,128)(2,1)S(1)} %get-tuple-element.69.e3, bf16[192,192]{1,0:T(8,128)(2,1)S(1)} %get-tuple-element.70.bwd1, bf16[14,64,128]{2,1,0:T(8,128)(2,1)S(1)} %get-tuple-element.71.mine_a, ...), custom_call_target="tpu_custom_call" | custom-call | flops 770000000 | tf_op jit(solution)/shard_map/input/pallas_call | solution.py:587
  13.8 0.5 %collective-permute-done.4.received = f32[8,4736]{1,0:T(8,128)S(1)} collective-permute-done((f32[8,4736]{1,0:T(8,128)S(1)}, f32[8,4736]{1,0:T(8,128)S(1)}, u32[]{:S(2)}, u32[]{:S(2)}) %collective-permute-start.4) | collective-permute-done | bytes 151584 | tf_op jit(solution)/shard_map/ppermute | solution.py:586
  14.6 2.1 %collective-permute-start.8 = (bf16[8,4736]{1,0:T(8,128)(2,1)S(1)}, bf16[8,4736]{1,0:T(8,128)(2,1)S(1)}, u32[]{:S(2)}, u32[]{:S(2)}) collective-permute-start(bf16[8,4736]{1,0:T(8,128)(2,1)S(1)} %get-tuple-element.83.refs_0_), channel_id=1, source_target_pairs={{0,24},{1,2},{2,1},{3,27},{4,7},{5,29},{6,30},{7,4},{8,11},{9,17},... | collective-permute-start | bytes 227336 | tf_op jit(solution)/shard_map/ppermute | solution.py:610
  16.7 1.1 %collective-permute-start.7 = (bf16[8,4736]{1,0:T(8,128)(2,1)S(1)}, bf16[8,4736]{1,0:T(8,128)(2,1)S(1)}, u32[]{:S(2)}, u32[]{:S(2)}) collective-permute-start(bf16[8,4736]{1,0:T(8,128)(2,1)S(1)} %get-tuple-element.83.refs_0_), channel_id=1, source_target_pairs={{0,20},{1,7},{2,4},{3,23},{4,2},{5,17},{6,18},{7,1},{8,14},{9,29},... | collective-permute-start | bytes 227336 | tf_op jit(solution)/shard_map/ppermute | solution.py:610
  17.9 1.3 %outputs.1 = (bf16[1,64,32,128]{3,2,1,0:T(8,128)(2,1)}, bf16[1,64,32,128]{3,2,1,0:T(8,128)(2,1)}, f32[8,128]{1,0:T(8,128)S(1)}) custom-call(bf16[32,64,128]{2,1,0:T(8,128)(2,1)S(1)} %get-tuple-element.75.mine, bf16[32,64,128]{2,1,0:T(8,128)(2,1)S(1)} %collective-permute-done.5.back), custom_call_target="tpu_custom_call" | custom-call | flops 1430000000 | tf_op jit(solution)/shard_map/outputs/pallas_call | solution.py:600
  19.1 0.8 %collective-permute-done.8.refs_3_ = bf16[8,4736]{1,0:T(8,128)(2,1)S(1)} collective-permute-done((bf16[8,4736]{1,0:T(8,128)(2,1)S(1)}, bf16[8,4736]{1,0:T(8,128)(2,1)S(1)}, u32[]{:S(2)}, u32[]{:S(2)}) %collective-permute-start.8) | collective-permute-done | bytes 75808 | tf_op jit(solution)/shard_map/ppermute | solution.py:610
  19.9 0.8 %collective-permute-done.7.refs_2_ = bf16[8,4736]{1,0:T(8,128)(2,1)S(1)} collective-permute-done((bf16[8,4736]{1,0:T(8,128)(2,1)S(1)}, bf16[8,4736]{1,0:T(8,128)(2,1)S(1)}, u32[]{:S(2)}, u32[]{:S(2)}) %collective-permute-start.7) | collective-permute-done | bytes 75808 | tf_op jit(solution)/shard_map/ppermute | solution.py:610
  20.7 0.9 %collective-permute-done.6.refs_1_ = bf16[8,4736]{1,0:T(8,128)(2,1)S(1)} collective-permute-done((bf16[8,4736]{1,0:T(8,128)(2,1)S(1)}, bf16[8,4736]{1,0:T(8,128)(2,1)S(1)}, u32[]{:S(2)}, u32[]{:S(2)}) %collective-permute-start.6) | collective-permute-done | bytes 75808 | tf_op jit(solution)/shard_map/ppermute | solution.py:610
  21.7 3.7 %collective-permute-start.11 = (bf16[8,4736]{1,0:T(8,128)(2,1)S(1)}, bf16[8,4736]{1,0:T(8,128)(2,1)S(1)}, u32[]{:S(2)}, u32[]{:S(2)}) collective-permute-start(bf16[8,4736]{1,0:T(8,128)(2,1)S(1)} %add.2.refs_0_), channel_id=1, source_target_pairs={{0,3},{1,25},{2,26},{3,0},{4,28},{5,6},{6,5},{7,31},{8,16},{9,10},... | collective-permute-start | bytes 227336 | tf_op jit(solution)/shard_map/ppermute | solution.py:610
  25.3 0.5 %collective-permute-start.9 = (bf16[8,4736]{1,0:T(8,128)(2,1)S(1)}, bf16[8,4736]{1,0:T(8,128)(2,1)S(1)}, u32[]{:S(2)}, u32[]{:S(2)}) collective-permute-start(bf16[8,4736]{1,0:T(8,128)(2,1)S(1)} %add.2.refs_0_), channel_id=1, source_target_pairs={{0,5},{1,13},{2,14},{3,6},{4,8},{5,0},{6,3},{7,11},{8,4},{9,12},{1... | collective-permute-start | bytes 227336 | tf_op jit(solution)/shard_map/ppermute | solution.py:610
  25.8 2.1 %collective-permute-done.11.refs_3_ = bf16[8,4736]{1,0:T(8,128)(2,1)S(1)} collective-permute-done((bf16[8,4736]{1,0:T(8,128)(2,1)S(1)}, bf16[8,4736]{1,0:T(8,128)(2,1)S(1)}, u32[]{:S(2)}, u32[]{:S(2)}) %collective-permute-start.11) | collective-permute-done | bytes 75808 | tf_op jit(solution)/shard_map/ppermute | solution.py:610
  27.9 2.5 %collective-permute-done.10.refs_2_ = bf16[8,4736]{1,0:T(8,128)(2,1)S(1)} collective-permute-done((bf16[8,4736]{1,0:T(8,128)(2,1)S(1)}, bf16[8,4736]{1,0:T(8,128)(2,1)S(1)}, u32[]{:S(2)}, u32[]{:S(2)}) %collective-permute-start.10) | collective-permute-done | bytes 75808 | tf_op jit(solution)/shard_map/ppermute | solution.py:610
  30.4 0.4 %collective-permute-start.12 = (f32[8,4736]{1,0:T(8,128)S(1)}, f32[8,4736]{1,0:T(8,128)S(1)}, u32[]{:S(2)}, u32[]{:S(2)}) collective-permute-start(f32[8,4736]{1,0:T(8,128)S(1)} %add.3.held), channel_id=1, source_target_pairs={{0,4},{4,0},{1,5},{5,1},{2,6},{6,2},{3,7},{7,3},{8,12},{12,8},{9,1... | collective-permute-start | bytes 454664 | tf_op jit(solution)/shard_map/ppermute | solution.py:618
  30.8 1.1 %collective-permute-done.12.swapped = f32[8,4736]{1,0:T(8,128)S(1)} collective-permute-done((f32[8,4736]{1,0:T(8,128)S(1)}, f32[8,4736]{1,0:T(8,128)S(1)}, u32[]{:S(2)}, u32[]{:S(2)}) %collective-permute-start.12) | collective-permute-done | bytes 151584 | tf_op jit(solution)/shard_map/ppermute | solution.py:618
  31.9 1.0 %grads.1 = (f32[3,3,64,64]{3,2,1,0:T(8,128)}, f32[1,64]{1,0:T(1,128)}, f32[3,3,64,64]{3,2,1,0:T(8,128)}, f32[1,64]{1,0:T(1,128)}) custom-call(f32[8,4736]{1,0:T(8,128)S(1)} %add.3.held, f32[8,4736]{1,0:T(8,128)S(1)} %collective-permute-done.12.swapped), custom_call_target="tpu_custom_call" | custom-call | tf_op jit(solution)/shard_map/grads/pallas_call | solution.py:621
  (13 shorter events, 0.8 us)
Async XLA Ops:
  0.6 5.5 %collective-permute-start = (bf16[1,64,32,128]{3,2,1,0:T(8,128)(2,1)}, bf16[1,64,32,128]{3,2,1,0:T(8,128)(2,1)S(1)}, u32[]{:S(2)}, u32[]{:S(2)}) collective-permute-start(bf16[1,64,32,128]{3,2,1,0:T(8,128)(2,1)} %image_ref.1), channel_id=1, source_target_pairs={{0,4},{4,0},{1,5},{5,1},{2,6},{6,2},{3,7},{7,3},{8,12},{12,8},{9,1... | collective-permute-start | bytes 1572872 | tf_op jit(solution)/shard_map/ppermute | solution.py:497
  1.2 4.9 %collective-permute-start.1 = (bf16[1,64,32,128]{3,2,1,0:T(8,128)(2,1)}, bf16[1,64,32,128]{3,2,1,0:T(8,128)(2,1)S(1)}, u32[]{:S(2)}, u32[]{:S(2)}) collective-permute-start(bf16[1,64,32,128]{3,2,1,0:T(8,128)(2,1)} %cot_ref.1), channel_id=1, source_target_pairs={{0,4},{4,0},{1,5},{5,1},{2,6},{6,2},{3,7},{7,3},{8,12},{12,8},{9,1... | collective-permute-start | bytes 1572872 | tf_op jit(solution)/shard_map/ppermute | solution.py:498
  2.7 7.8 %collective-permute-start.3 = (bf16[6,64,128]{2,1,0:T(8,128)(2,1)S(1)}, bf16[6,64,128]{2,1,0:T(8,128)(2,1)S(1)}, u32[]{:S(2)}, u32[]{:S(2)}) collective-permute-start(bf16[6,64,128]{2,1,0:T(8,128)(2,1)S(1)} %get-tuple-element.48), channel_id=1, source_target_pairs={{0,1},{4,8},{1,0},{5,9},{2,3},{6,10},{3,2},{7,11},{8,4},{12,16},{9... | collective-permute-start | bytes 294920 | tf_op jit(solution)/shard_map/ppermute | solution.py:535
  6.5 4.7 %collective-permute-start.2 = (bf16[6,64,128]{2,1,0:T(8,128)(2,1)S(1)}, bf16[6,64,128]{2,1,0:T(8,128)(2,1)S(1)}, u32[]{:S(2)}, u32[]{:S(2)}) collective-permute-start(bf16[6,64,128]{2,1,0:T(8,128)(2,1)S(1)} %get-tuple-element.47), channel_id=1, source_target_pairs={{0,1},{4,8},{1,0},{5,9},{2,3},{6,10},{3,2},{7,11},{8,4},{12,16},{9... | collective-permute-start | bytes 294920 | tf_op jit(solution)/shard_map/ppermute | solution.py:536
  12.9 1.4 %collective-permute-start.4 = (f32[8,4736]{1,0:T(8,128)S(1)}, f32[8,4736]{1,0:T(8,128)S(1)}, u32[]{:S(2)}, u32[]{:S(2)}) collective-permute-start(f32[8,4736]{1,0:T(8,128)S(1)} %get-tuple-element.78), channel_id=1, source_target_pairs={{0,4},{4,0},{1,5},{5,1},{2,6},{6,2},{3,7},{7,3},{8,12},{12,8},{9,1... | collective-permute-start | bytes 454664 | tf_op jit(solution)/shard_map/ppermute | solution.py:586
  14.3 3.5 %collective-permute-start.5 = (bf16[32,64,128]{2,1,0:T(8,128)(2,1)S(1)}, bf16[32,64,128]{2,1,0:T(8,128)(2,1)S(1)}, u32[]{:S(2)}, u32[]{:S(2)}) collective-permute-start(bf16[32,64,128]{2,1,0:T(8,128)(2,1)S(1)} %get-tuple-element.79), channel_id=1, source_target_pairs={{0,4},{4,0},{1,5},{5,1},{2,6},{6,2},{3,7},{7,3},{8,12},{12,8},{9,1... | collective-permute-start | bytes 1572872 | tf_op jit(solution)/shard_map/ppermute | solution.py:599
  14.6 5.3 %collective-permute-start.8 = (bf16[8,4736]{1,0:T(8,128)(2,1)S(1)}, bf16[8,4736]{1,0:T(8,128)(2,1)S(1)}, u32[]{:S(2)}, u32[]{:S(2)}) collective-permute-start(bf16[8,4736]{1,0:T(8,128)(2,1)S(1)} %get-tuple-element.83.refs_0_), channel_id=1, source_target_pairs={{0,24},{1,2},{2,1},{3,27},{4,7},{5,29},{6,30},{7,4},{8,11},{9,17},... | collective-permute-start | bytes 227336 | tf_op jit(solution)/shard_map/ppermute | solution.py:610
  16.7 4.0 %collective-permute-start.7 = (bf16[8,4736]{1,0:T(8,128)(2,1)S(1)}, bf16[8,4736]{1,0:T(8,128)(2,1)S(1)}, u32[]{:S(2)}, u32[]{:S(2)}) collective-permute-start(bf16[8,4736]{1,0:T(8,128)(2,1)S(1)} %get-tuple-element.83.refs_0_), channel_id=1, source_target_pairs={{0,20},{1,7},{2,4},{3,23},{4,2},{5,17},{6,18},{7,1},{8,14},{9,29},... | collective-permute-start | bytes 227336 | tf_op jit(solution)/shard_map/ppermute | solution.py:610
  17.8 3.8 %collective-permute-start.6 = (bf16[8,4736]{1,0:T(8,128)(2,1)S(1)}, bf16[8,4736]{1,0:T(8,128)(2,1)S(1)}, u32[]{:S(2)}, u32[]{:S(2)}) collective-permute-start(bf16[8,4736]{1,0:T(8,128)(2,1)S(1)} %get-tuple-element.83.refs_0_), channel_id=1, source_target_pairs={{0,12},{1,4},{2,7},{3,15},{4,1},{5,9},{6,10},{7,2},{8,13},{9,5},{1... | collective-permute-start | bytes 227336 | tf_op jit(solution)/shard_map/ppermute | solution.py:610
  21.7 6.2 %collective-permute-start.11 = (bf16[8,4736]{1,0:T(8,128)(2,1)S(1)}, bf16[8,4736]{1,0:T(8,128)(2,1)S(1)}, u32[]{:S(2)}, u32[]{:S(2)}) collective-permute-start(bf16[8,4736]{1,0:T(8,128)(2,1)S(1)} %add.2.refs_0_), channel_id=1, source_target_pairs={{0,3},{1,25},{2,26},{3,0},{4,28},{5,6},{6,5},{7,31},{8,16},{9,10},... | collective-permute-start | bytes 227336 | tf_op jit(solution)/shard_map/ppermute | solution.py:610
  25.3 5.0 %collective-permute-start.10 = (bf16[8,4736]{1,0:T(8,128)(2,1)S(1)}, bf16[8,4736]{1,0:T(8,128)(2,1)S(1)}, u32[]{:S(2)}, u32[]{:S(2)}) collective-permute-start(bf16[8,4736]{1,0:T(8,128)(2,1)S(1)} %add.2.refs_0_), channel_id=1, source_target_pairs={{0,6},{1,21},{2,22},{3,5},{4,16},{5,3},{6,0},{7,19},{8,28},{9,15},... | collective-permute-start | bytes 227336 | tf_op jit(solution)/shard_map/ppermute | solution.py:610
  25.3 5.0 %collective-permute-start.9 = (bf16[8,4736]{1,0:T(8,128)(2,1)S(1)}, bf16[8,4736]{1,0:T(8,128)(2,1)S(1)}, u32[]{:S(2)}, u32[]{:S(2)}) collective-permute-start(bf16[8,4736]{1,0:T(8,128)(2,1)S(1)} %add.2.refs_0_), channel_id=1, source_target_pairs={{0,5},{1,13},{2,14},{3,6},{4,8},{5,0},{6,3},{7,11},{8,4},{9,12},{1... | collective-permute-start | bytes 227336 | tf_op jit(solution)/shard_map/ppermute | solution.py:610
  30.4 1.4 %collective-permute-start.12 = (f32[8,4736]{1,0:T(8,128)S(1)}, f32[8,4736]{1,0:T(8,128)S(1)}, u32[]{:S(2)}, u32[]{:S(2)}) collective-permute-start(f32[8,4736]{1,0:T(8,128)S(1)} %add.3.held), channel_id=1, source_target_pairs={{0,4},{4,0},{1,5},{5,1},{2,6},{6,2},{3,7},{7,3},{8,12},{12,8},{9,1... | collective-permute-start | bytes 454664 | tf_op jit(solution)/shard_map/ppermute | solution.py:618

commit v5 on v3

--- a/solution.py
+++ b/solution.py
@@ -423,23 +423,30 @@
     token[...] = jnp.zeros(token.shape, F32)
 
 
-def grads_kernel(held, swapped, gw1, gb1, gw2, gb2):
+def grads_kernel(held, swapped, gw1, gb1, gw2, gb2, gw1_v, gw2_v, sems):
     own = own_half()
 
     def tile(part, t):
         at = slice(128 * t, 128 * t + 128)
         return jnp.where(own == part, held[:, at], swapped[:, at])
 
-    for block in range(24):
-        part, first = block // 12, 3 * (block % 12)
-        line = jnp.concatenate([tile(part, first + p) for p in range(3)], axis=1)
-        b, i = block // 8, (block % 8) * 8
-        for a in range(3):
-            gw2[a, b, i : i + 8, :] = line[:, a * 64 : a * 64 + 64]
-            gw1[a, b, i : i + 8, :] = line[:, 192 + a * 64 : 256 + a * 64]
+    copies = []
+    for layer, buffer, out in ((0, gw2_v, gw2), (1, gw1_v, gw1)):
+        for block in range(24):
+            part, first = block // 12, 3 * (block % 12) + layer
+            pair = jnp.concatenate([tile(part, first), tile(part, first + 1)], axis=1)
+            b, i = block // 8, (block % 8) * 8
+            for a in range(3):
+                at = 64 * layer + 64 * a
+                buffer[a, b, i : i + 8, :] = pair[:, at : at + 64]
+        copy = pltpu.make_async_copy(buffer, out, sems.at[layer])
+        copy.start()
+        copies.append(copy)
     biases = tile(0, 36)
     gb2[...] = biases[0:1, 0:64]
     gb1[...] = biases[0:1, 64:128]
+    for copy in copies:
+        copy.wait()
 
 
 def exchange_stages(places, planes):
@@ -603,6 +610,12 @@
     gw1, gb1, gw2, gb2 = call(
         grads_kernel,
         out_shape=[weight_shape, bias_shape, weight_shape, bias_shape],
+        out_specs=[pl.BlockSpec(memory_space=m) for m in (pltpu.HBM, pltpu.VMEM) * 2],
+        scratch_shapes=[
+            pltpu.VMEM((3, 3, chans, chans), F32),
+            pltpu.VMEM((3, 3, chans, chans), F32),
+            pltpu.SemaphoreType.DMA((2,)),
+        ],
         name="grads",
     )(*near(held, swapped_sums))
     return out, image_grad, gw1, gb1.reshape(chans), gw2, gb2.reshape(chans)

time: 32.5 us -> 33 us (1.015)
  Pallas kernels: 9.92 us -> 10.4 us
    pallas_call x1, Pallas kernels: 0.97 us -> 1.44 us  [local(): call(grads_kernel, out_shape=[weight_shape, bias_shape, weight_shape, bia...]
where the time goes in v5:
time: 33 us; the launch traced here: 32.9 us
  starting transfers between devices  13 us (39%)
  Pallas kernels  10.4 us (32%)
  waiting for transfers between devices  8.79 us (27%)
  between operations  0.72 us (2%)
    ppermute x6, starting transfers between devices, local(): received = [lax.ppermute(held, axes, pairs) for pairs in stage]  7.38 us
    ppermute x6, waiting for transfers between devices, local(): received = [lax.ppermute(held, axes, pairs) for pairs in stage]  7.02 us
    pallas_call x1, Pallas kernels, local(): call(inner_kernel, out_shape=[flat(208, half + 4), flat(208, half + 2), f...  3.44 us
    ppermute x1, starting transfers between devices, local(): edges_other = lax.ppermute(edges, axes, across)  2.65 us
    ppermute x1, starting transfers between devices, local(): edges_own = lax.ppermute(swapped[half:half + 6], axes, across)  1.72 us
    pallas_call x1, Pallas kernels, local(): call(outer_kernel, out_shape=[flat(192, 4), rows_of(2), rows_of(2), half_...  1.69 us
    pallas_call x1, Pallas kernels, local(): call(pack_kernel, out_shape=[rows_of(rows), rows_of(rows), rows_of(2 * ha...  1.53 us
    pallas_call x1, Pallas kernels, local(): call(grads_kernel, out_shape=[weight_shape, bias_shape, weight_shape, bia...  1.44 us
  transfers between devices with their start and end apart: 12, of which 7 were waited for; matrix products, arithmetic and copies ran while one was open for 0% of the time, Pallas kernels for 17%

profile of v5, /device:TPU:0, one launch (start us, length us, event | category | flops | bytes accessed | tf_op | source)
XLA Modules:
  0.0 32.9 jit_solution(7243364073415486275)
XLA Ops:
  0.6 1.5 %pack.1 = (bf16[32,64,128]{2,1,0:T(8,128)(2,1)S(1)}, bf16[32,64,128]{2,1,0:T(8,128)(2,1)S(1)}, bf16[38,64,128]{2,1,0:T(8,128)(2,1)S(1)}, bf16[6,64,128]{2,1,0:T(...) custom-call(bf16[1,64,32,128]{3,2,1,0:T(8,128)(2,1)} %image_ref.1, ...), custom_call_target="tpu_custom_call" | custom-call | tf_op jit(solution)/shard_map/pack/pallas_call | solution.py:493
  2.2 0.5 %collective-permute-start = (bf16[38,64,128]{2,1,0:T(8,128)(2,1)S(1)}, bf16[38,64,128]{2,1,0:T(8,128)(2,1)S(1)}, u32[]{:S(2)}, u32[]{:S(2)}) collective-permute-start(bf16[38,64,128]{2,1,0:T(8,128)(2,1)S(1)} %get-tuple-element.45), channel_id=1, source_target_pairs={{0,4},{4,0},{1,5},{5,1},{2,6},{6,2},{3,7},{7,3},{8,12},{12,8},{9,1... | collective-permute-start | bytes 1867784 | tf_op jit(solution)/shard_map/ppermute | solution.py:516
  2.7 2.6 %collective-permute-start.2 = (bf16[6,64,128]{2,1,0:T(8,128)(2,1)S(1)}, bf16[6,64,128]{2,1,0:T(8,128)(2,1)S(1)}, u32[]{:S(2)}, u32[]{:S(2)}) collective-permute-start(bf16[6,64,128]{2,1,0:T(8,128)(2,1)S(1)} %get-tuple-element.46), channel_id=1, source_target_pairs={{0,1},{4,8},{1,0},{5,9},{2,3},{6,10},{3,2},{7,11},{8,4},{12,16},{9... | collective-permute-start | bytes 294920 | tf_op jit(solution)/shard_map/ppermute | solution.py:524
  5.3 0.3 weights.1
  5.7 1.7 %collective-permute-start.1 = (bf16[6,64,128]{2,1,0:T(8,128)(2,1)S(1)}, bf16[6,64,128]{2,1,0:T(8,128)(2,1)S(1)}, u32[]{:S(2)}, u32[]{:S(2)}) collective-permute-start(bf16[6,64,128]{2,1,0:T(8,128)(2,1)S(1)} %slice.4), channel_id=1, source_target_pairs={{0,1},{4,8},{1,0},{5,9},{2,3},{6,10},{3,2},{7,11},{8,4},{12,16},{9... | collective-permute-start | bytes 294920 | tf_op jit(solution)/shard_map/ppermute | solution.py:525
  7.4 3.4 %inner.1 = (bf16[208,5120]{1,0:T(8,128)(2,1)S(1)}, bf16[208,4608]{1,0:T(8,128)(2,1)S(1)}, bf16[192,4096]{1,0:T(8,128)(2,1)S(1)}, bf16[192,3584]{1,0:T(8,128)(2,1...) custom-call(bf16[32,64,128]{2,1,0:T(8,128)(2,1)S(1)} %get-tuple-elem, ...), custom_call_target="tpu_custom_call" | custom-call | flops 4400000000 | tf_op jit(solution)/shard_map/inner/pallas_call | solution.py:533
  10.9 1.7 %outer.1 = (bf16[192,1024]{1,0:T(8,128)(2,1)S(1)}, bf16[2,64,128]{2,1,0:T(8,128)(2,1)S(1)}, bf16[2,64,128]{2,1,0:T(8,128)(2,1)S(1)}, f32[8,4736]{1,0:T(8,128)S(1)}, f32[8,4736]{1,0:T(8,128)S(1)}) custom-call(bf16[6,64,128]{2,1,0:T(8,128)(2,1)S(1)} %collective-permute-done.1.edges_own, bf16[6,64,128]{2,1,0:T(8,128)(2,1)S(1)} %collective-permute-done.2.edges_other, ...), custom_call_target="tpu_custom_call" | custom-call | flops 2200000000 | tf_op jit(solution)/shard_map/outer/pallas_call | solution.py:556
  12.6 0.1 collective-permute-start.3
  12.7 0.6 %input.1 = (bf16[32,64,128]{2,1,0:T(8,128)(2,1)S(1)}, bf16[32,64,128]{2,1,0:T(8,128)(2,1)S(1)}) custom-call(bf16[192,1024]{1,0:T(8,128)(2,1)S(1)} %get-tuple-element.64.e3_b, bf16[192,3584]{1,0:T(8,128)(2,1)S(1)} %get-tuple-element.65.e3, bf16[192,192]{1,0:T(8,128)(2,1)S(1)} %get-tuple-element.66.bwd1, bf16[14,64,128]{2,1,0:T(8,128)(2,1)S(1)} %get-tuple-element.67.mine_a, ...), custom_call_target="tpu_custom_call" | custom-call | flops 770000000 | tf_op jit(solution)/shard_map/input/pallas_call | solution.py:576
  13.3 0.7 %collective-permute-done.3.received = f32[8,4736]{1,0:T(8,128)S(1)} collective-permute-done((f32[8,4736]{1,0:T(8,128)S(1)}, f32[8,4736]{1,0:T(8,128)S(1)}, u32[]{:S(2)}, u32[]{:S(2)}) %collective-permute-start.3) | collective-permute-done | bytes 151584 | tf_op jit(solution)/shard_map/ppermute | solution.py:575
  14.0 0.2 collective-permute-start.4
  14.2 2.4 %collective-permute-start.7 = (bf16[8,4736]{1,0:T(8,128)(2,1)S(1)}, bf16[8,4736]{1,0:T(8,128)(2,1)S(1)}, u32[]{:S(2)}, u32[]{:S(2)}) collective-permute-start(bf16[8,4736]{1,0:T(8,128)(2,1)S(1)} %get-tuple-element.79.refs_0_), channel_id=1, source_target_pairs={{0,24},{1,2},{2,1},{3,27},{4,7},{5,29},{6,30},{7,4},{8,11},{9,17},... | collective-permute-start | bytes 227336 | tf_op jit(solution)/shard_map/ppermute | solution.py:599
  16.6 0.8 %collective-permute-start.6 = (bf16[8,4736]{1,0:T(8,128)(2,1)S(1)}, bf16[8,4736]{1,0:T(8,128)(2,1)S(1)}, u32[]{:S(2)}, u32[]{:S(2)}) collective-permute-start(bf16[8,4736]{1,0:T(8,128)(2,1)S(1)} %get-tuple-element.79.refs_0_), channel_id=1, source_target_pairs={{0,20},{1,7},{2,4},{3,23},{4,2},{5,17},{6,18},{7,1},{8,14},{9,29},... | collective-permute-start | bytes 227336 | tf_op jit(solution)/shard_map/ppermute | solution.py:599
  17.4 1.3 %outputs.1 = (bf16[1,64,32,128]{3,2,1,0:T(8,128)(2,1)}, bf16[1,64,32,128]{3,2,1,0:T(8,128)(2,1)}, f32[8,128]{1,0:T(8,128)S(1)}) custom-call(bf16[32,64,128]{2,1,0:T(8,128)(2,1)S(1)} %get-tuple-element.71.mine, bf16[32,64,128]{2,1,0:T(8,128)(2,1)S(1)} %collective-permute-done.4.back), custom_call_target="tpu_custom_call" | custom-call | flops 1430000000 | tf_op jit(solution)/shard_map/outputs/pallas_call | solution.py:589
  18.7 0.8 %collective-permute-done.7.refs_3_ = bf16[8,4736]{1,0:T(8,128)(2,1)S(1)} collective-permute-done((bf16[8,4736]{1,0:T(8,128)(2,1)S(1)}, bf16[8,4736]{1,0:T(8,128)(2,1)S(1)}, u32[]{:S(2)}, u32[]{:S(2)}) %collective-permute-start.7) | collective-permute-done | bytes 75808 | tf_op jit(solution)/shard_map/ppermute | solution.py:599
  19.5 0.9 %collective-permute-done.6.refs_2_ = bf16[8,4736]{1,0:T(8,128)(2,1)S(1)} collective-permute-done((bf16[8,4736]{1,0:T(8,128)(2,1)S(1)}, bf16[8,4736]{1,0:T(8,128)(2,1)S(1)}, u32[]{:S(2)}, u32[]{:S(2)}) %collective-permute-start.6) | collective-permute-done | bytes 75808 | tf_op jit(solution)/shard_map/ppermute | solution.py:599
  20.4 0.8 %collective-permute-done.5.refs_1_ = bf16[8,4736]{1,0:T(8,128)(2,1)S(1)} collective-permute-done((bf16[8,4736]{1,0:T(8,128)(2,1)S(1)}, bf16[8,4736]{1,0:T(8,128)(2,1)S(1)}, u32[]{:S(2)}, u32[]{:S(2)}) %collective-permute-start.5) | collective-permute-done | bytes 75808 | tf_op jit(solution)/shard_map/ppermute | solution.py:599
  21.2 3.7 %collective-permute-start.10 = (bf16[8,4736]{1,0:T(8,128)(2,1)S(1)}, bf16[8,4736]{1,0:T(8,128)(2,1)S(1)}, u32[]{:S(2)}, u32[]{:S(2)}) collective-permute-start(bf16[8,4736]{1,0:T(8,128)(2,1)S(1)} %add.2.refs_0_), channel_id=1, source_target_pairs={{0,3},{1,25},{2,26},{3,0},{4,28},{5,6},{6,5},{7,31},{8,16},{9,10},... | collective-permute-start | bytes 227336 | tf_op jit(solution)/shard_map/ppermute | solution.py:599
  24.9 0.5 %collective-permute-start.8 = (bf16[8,4736]{1,0:T(8,128)(2,1)S(1)}, bf16[8,4736]{1,0:T(8,128)(2,1)S(1)}, u32[]{:S(2)}, u32[]{:S(2)}) collective-permute-start(bf16[8,4736]{1,0:T(8,128)(2,1)S(1)} %add.2.refs_0_), channel_id=1, source_target_pairs={{0,5},{1,13},{2,14},{3,6},{4,8},{5,0},{6,3},{7,11},{8,4},{9,12},{1... | collective-permute-start | bytes 227336 | tf_op jit(solution)/shard_map/ppermute | solution.py:599
  25.4 2.1 %collective-permute-done.10.refs_3_ = bf16[8,4736]{1,0:T(8,128)(2,1)S(1)} collective-permute-done((bf16[8,4736]{1,0:T(8,128)(2,1)S(1)}, bf16[8,4736]{1,0:T(8,128)(2,1)S(1)}, u32[]{:S(2)}, u32[]{:S(2)}) %collective-permute-start.10) | collective-permute-done | bytes 75808 | tf_op jit(solution)/shard_map/ppermute | solution.py:599
  27.5 2.5 %collective-permute-done.9.refs_2_ = bf16[8,4736]{1,0:T(8,128)(2,1)S(1)} collective-permute-done((bf16[8,4736]{1,0:T(8,128)(2,1)S(1)}, bf16[8,4736]{1,0:T(8,128)(2,1)S(1)}, u32[]{:S(2)}, u32[]{:S(2)}) %collective-permute-start.9) | collective-permute-done | bytes 75808 | tf_op jit(solution)/shard_map/ppermute | solution.py:599
  30.0 0.4 %collective-permute-start.11 = (f32[8,4736]{1,0:T(8,128)S(1)}, f32[8,4736]{1,0:T(8,128)S(1)}, u32[]{:S(2)}, u32[]{:S(2)}) collective-permute-start(f32[8,4736]{1,0:T(8,128)S(1)} %add.3.held), channel_id=1, source_target_pairs={{0,4},{4,0},{1,5},{5,1},{2,6},{6,2},{3,7},{7,3},{8,12},{12,8},{9,1... | collective-permute-start | bytes 454664 | tf_op jit(solution)/shard_map/ppermute | solution.py:607
  30.3 1.1 %collective-permute-done.11.swapped = f32[8,4736]{1,0:T(8,128)S(1)} collective-permute-done((f32[8,4736]{1,0:T(8,128)S(1)}, f32[8,4736]{1,0:T(8,128)S(1)}, u32[]{:S(2)}, u32[]{:S(2)}) %collective-permute-start.11) | collective-permute-done | bytes 151584 | tf_op jit(solution)/shard_map/ppermute | solution.py:607
  31.4 1.4 %grads.1 = (f32[3,3,64,64]{3,2,1,0:T(8,128)}, f32[1,64]{1,0:T(1,128)}, f32[3,3,64,64]{3,2,1,0:T(8,128)}, f32[1,64]{1,0:T(1,128)}) custom-call(f32[8,4736]{1,0:T(8,128)S(1)} %add.3.held, f32[8,4736]{1,0:T(8,128)S(1)} %collective-permute-done.11.swapped), custom_call_target="tpu_custom_call" | custom-call | tf_op jit(solution)/shard_map/grads/pallas_call | solution.py:610
  (11 shorter events, 0.2 us)
Async XLA Ops:
  2.2 3.5 %collective-permute-start = (bf16[38,64,128]{2,1,0:T(8,128)(2,1)S(1)}, bf16[38,64,128]{2,1,0:T(8,128)(2,1)S(1)}, u32[]{:S(2)}, u32[]{:S(2)}) collective-permute-start(bf16[38,64,128]{2,1,0:T(8,128)(2,1)S(1)} %get-tuple-element.45), channel_id=1, source_target_pairs={{0,4},{4,0},{1,5},{5,1},{2,6},{6,2},{3,7},{7,3},{8,12},{12,8},{9,1... | collective-permute-start | bytes 1867784 | tf_op jit(solution)/shard_map/ppermute | solution.py:516
  2.7 8.1 %collective-permute-start.2 = (bf16[6,64,128]{2,1,0:T(8,128)(2,1)S(1)}, bf16[6,64,128]{2,1,0:T(8,128)(2,1)S(1)}, u32[]{:S(2)}, u32[]{:S(2)}) collective-permute-start(bf16[6,64,128]{2,1,0:T(8,128)(2,1)S(1)} %get-tuple-element.46), channel_id=1, source_target_pairs={{0,1},{4,8},{1,0},{5,9},{2,3},{6,10},{3,2},{7,11},{8,4},{12,16},{9... | collective-permute-start | bytes 294920 | tf_op jit(solution)/shard_map/ppermute | solution.py:524
  5.7 5.2 %collective-permute-start.1 = (bf16[6,64,128]{2,1,0:T(8,128)(2,1)S(1)}, bf16[6,64,128]{2,1,0:T(8,128)(2,1)S(1)}, u32[]{:S(2)}, u32[]{:S(2)}) collective-permute-start(bf16[6,64,128]{2,1,0:T(8,128)(2,1)S(1)} %slice.4), channel_id=1, source_target_pairs={{0,1},{4,8},{1,0},{5,9},{2,3},{6,10},{3,2},{7,11},{8,4},{12,16},{9... | collective-permute-start | bytes 294920 | tf_op jit(solution)/shard_map/ppermute | solution.py:525
  12.6 1.4 %collective-permute-start.3 = (f32[8,4736]{1,0:T(8,128)S(1)}, f32[8,4736]{1,0:T(8,128)S(1)}, u32[]{:S(2)}, u32[]{:S(2)}) collective-permute-start(f32[8,4736]{1,0:T(8,128)S(1)} %get-tuple-element.74), channel_id=1, source_target_pairs={{0,4},{4,0},{1,5},{5,1},{2,6},{6,2},{3,7},{7,3},{8,12},{12,8},{9,1... | collective-permute-start | bytes 454664 | tf_op jit(solution)/shard_map/ppermute | solution.py:575
  14.0 3.4 %collective-permute-start.4 = (bf16[32,64,128]{2,1,0:T(8,128)(2,1)S(1)}, bf16[32,64,128]{2,1,0:T(8,128)(2,1)S(1)}, u32[]{:S(2)}, u32[]{:S(2)}) collective-permute-start(bf16[32,64,128]{2,1,0:T(8,128)(2,1)S(1)} %get-tuple-element.75), channel_id=1, source_target_pairs={{0,4},{4,0},{1,5},{5,1},{2,6},{6,2},{3,7},{7,3},{8,12},{12,8},{9,1... | collective-permute-start | bytes 1572872 | tf_op jit(solution)/shard_map/ppermute | solution.py:588
  14.2 5.3 %collective-permute-start.7 = (bf16[8,4736]{1,0:T(8,128)(2,1)S(1)}, bf16[8,4736]{1,0:T(8,128)(2,1)S(1)}, u32[]{:S(2)}, u32[]{:S(2)}) collective-permute-start(bf16[8,4736]{1,0:T(8,128)(2,1)S(1)} %get-tuple-element.79.refs_0_), channel_id=1, source_target_pairs={{0,24},{1,2},{2,1},{3,27},{4,7},{5,29},{6,30},{7,4},{8,11},{9,17},... | collective-permute-start | bytes 227336 | tf_op jit(solution)/shard_map/ppermute | solution.py:599
  16.6 3.8 %collective-permute-start.6 = (bf16[8,4736]{1,0:T(8,128)(2,1)S(1)}, bf16[8,4736]{1,0:T(8,128)(2,1)S(1)}, u32[]{:S(2)}, u32[]{:S(2)}) collective-permute-start(bf16[8,4736]{1,0:T(8,128)(2,1)S(1)} %get-tuple-element.79.refs_0_), channel_id=1, source_target_pairs={{0,20},{1,7},{2,4},{3,23},{4,2},{5,17},{6,18},{7,1},{8,14},{9,29},... | collective-permute-start | bytes 227336 | tf_op jit(solution)/shard_map/ppermute | solution.py:599
  17.4 3.8 %collective-permute-start.5 = (bf16[8,4736]{1,0:T(8,128)(2,1)S(1)}, bf16[8,4736]{1,0:T(8,128)(2,1)S(1)}, u32[]{:S(2)}, u32[]{:S(2)}) collective-permute-start(bf16[8,4736]{1,0:T(8,128)(2,1)S(1)} %get-tuple-element.79.refs_0_), channel_id=1, source_target_pairs={{0,12},{1,4},{2,7},{3,15},{4,1},{5,9},{6,10},{7,2},{8,13},{9,5},{1... | collective-permute-start | bytes 227336 | tf_op jit(solution)/shard_map/ppermute | solution.py:599
  21.2 6.2 %collective-permute-start.10 = (bf16[8,4736]{1,0:T(8,128)(2,1)S(1)}, bf16[8,4736]{1,0:T(8,128)(2,1)S(1)}, u32[]{:S(2)}, u32[]{:S(2)}) collective-permute-start(bf16[8,4736]{1,0:T(8,128)(2,1)S(1)} %add.2.refs_0_), channel_id=1, source_target_pairs={{0,3},{1,25},{2,26},{3,0},{4,28},{5,6},{6,5},{7,31},{8,16},{9,10},... | collective-permute-start | bytes 227336 | tf_op jit(solution)/shard_map/ppermute | solution.py:599
  24.9 5.0 %collective-permute-start.9 = (bf16[8,4736]{1,0:T(8,128)(2,1)S(1)}, bf16[8,4736]{1,0:T(8,128)(2,1)S(1)}, u32[]{:S(2)}, u32[]{:S(2)}) collective-permute-start(bf16[8,4736]{1,0:T(8,128)(2,1)S(1)} %add.2.refs_0_), channel_id=1, source_target_pairs={{0,6},{1,21},{2,22},{3,5},{4,16},{5,3},{6,0},{7,19},{8,28},{9,15},... | collective-permute-start | bytes 227336 | tf_op jit(solution)/shard_map/ppermute | solution.py:599
  24.9 5.0 %collective-permute-start.8 = (bf16[8,4736]{1,0:T(8,128)(2,1)S(1)}, bf16[8,4736]{1,0:T(8,128)(2,1)S(1)}, u32[]{:S(2)}, u32[]{:S(2)}) collective-permute-start(bf16[8,4736]{1,0:T(8,128)(2,1)S(1)} %add.2.refs_0_), channel_id=1, source_target_pairs={{0,5},{1,13},{2,14},{3,6},{4,8},{5,0},{6,3},{7,11},{8,4},{9,12},{1... | collective-permute-start | bytes 227336 | tf_op jit(solution)/shard_map/ppermute | solution.py:599
  30.0 1.4 %collective-permute-start.11 = (f32[8,4736]{1,0:T(8,128)S(1)}, f32[8,4736]{1,0:T(8,128)S(1)}, u32[]{:S(2)}, u32[]{:S(2)}) collective-permute-start(f32[8,4736]{1,0:T(8,128)S(1)} %add.3.held), channel_id=1, source_target_pairs={{0,4},{4,0},{1,5},{5,1},{2,6},{6,2},{3,7},{7,3},{8,12},{12,8},{9,1... | collective-permute-start | bytes 454664 | tf_op jit(solution)/shard_map/ppermute | solution.py:607
